TPU v7x, 128 devices: a whole 4x4x4 slice. The times are simulated.
128 devices in a mesh: row: 4 (over y), gz: 2 (over x_lo), vert: 16 (over z, x_hi, core).
Axes of the slice: x: 4 (x_hi: 2, x_lo: 2; x = x_hi * 2 + x_lo), y: 4, z: 4, core: 2. Of those that a mesh axis runs over, the one named last changes fastest.
Arguments:
- distribution: float32 [32, 32, 110592], P('row', 'gz', 'vert'), may hold values from 0 to 10, as said below
- z_order: int32 [48], P('vert'), may hold values from 0 to 47, as said below
- edge_codes: int32 [2, 4], P(None, 'row'), may hold values from 0 to 2, as said below
Outputs:
- new_distribution: float32 [32, 32, 110592], P('row', 'gz', 'vert')
- macroscopic: float32 [8, 32, 32], P(None, 'row', 'gz')
- boundary_flux: float32 [2, 32], P('gz', 'row')
Inputs may be any that keep to these rules, and one draw needn't show every extreme that they name: `z_order`: a permutation of 0 to 47. `edge_codes`: row 0 holds 0 (diffuse wall) or 1 (evaporating film), row 1 holds 0 (diffuse wall) or 2 (outflow); the first column's bottom is film and the last column's top is outflow. `distribution`: every entry is positive.
All inputs are finite; a program needn't handle non-finite values.
Results may differ from a plain program's by a relative error of at most 0.0003.
Values sent between devices are 32-bit elements; how exact they have to be, the bound alone decides.
A program may use at most 128 MiB of HBM per device.

v0:
```python
import math

import jax
import jax.numpy as jnp
import numpy as np
from jax import lax
from jax.sharding import PartitionSpec as P

NODES = 8
NVR = 48
NVT = 48
NVZ = 48
STEPS = 2


ELEMENT_WIDTH = 4.0
TIME_STEP = 0.001
KNUDSEN = 0.005
VISCOUS_RATIO = 2.0 / 3.0
SAT_DENSITY = 1.5
SPEED_LIMIT = 5.0
HIGHEST_PRECISION = lax.Precision.HIGHEST


def with_halo(cells, sides, width):
    for axis, dim in sides:
        count = lax.axis_size(axis)
        ends = count - 1
        head = lax.slice_in_dim(cells, 0, width, axis=dim)
        tail = lax.slice_in_dim(cells, cells.shape[dim] - width, cells.shape[dim], axis=dim)
        cells = jnp.concatenate(
            [
                lax.ppermute(tail, axis, [(i, (i + 1) % count) for i in range(ends)]),
                cells,
                lax.ppermute(head, axis, [((i + 1) % count, i) for i in range(ends)]),
            ],
            axis=dim,
        )
    return cells


def legendre_pair(position, point_count):
    previous = 1.0
    current = position
    for degree in range(2, point_count + 1):
        previous, current = (
            current,
            ((2 * degree - 1) * position * current - (degree - 1) * previous) / degree,
        )
    slope = point_count * (position * current - previous) / (position * position - 1.0)
    return (current, slope)


def dg_tables(point_count):
    point_list = []
    weight_list = []
    for number in range(point_count):
        position = math.cos(math.pi * (number + 0.75) / (point_count + 0.5))
        for sweep in range(60):
            value, slope = legendre_pair(position, point_count)
            position = position - value / slope
        value, slope = legendre_pair(position, point_count)
        point_list.append(position)
        weight_list.append(2.0 / ((1.0 - position * position) * slope * slope))
    point_list = point_list[::-1]
    weight_list = weight_list[::-1]
    products = []
    for row_number in range(point_count):
        product_value = 1.0
        for other in range(point_count):
            if other != row_number:
                product_value = product_value * (point_list[row_number] - point_list[other])
        products.append(product_value)
    derivative_rows = []
    for row_number in range(point_count):
        entries = []
        for column in range(point_count):
            if column == row_number:
                total_value = 0.0
                for other in range(point_count):
                    if other != row_number:
                        total_value = total_value + 1.0 / (
                            point_list[row_number] - point_list[other]
                        )
                entries.append(total_value)
            else:
                entries.append(
                    products[row_number]
                    / products[column]
                    / (point_list[row_number] - point_list[column])
                )
        derivative_rows.append(entries)
    right_list = []
    left_list = []
    for column in range(point_count):
        right_value = 1.0
        left_value = 1.0
        for other in range(point_count):
            if other != column:
                right_value = right_value * (1.0 - point_list[other])
                left_value = left_value * (-1.0 - point_list[other])
        right_list.append(right_value / products[column])
        left_list.append(left_value / products[column])
    points = np.array(point_list)
    quad_weights = np.array(weight_list)
    derivative = np.array(derivative_rows)
    end_right = np.array(right_list)
    end_left = np.array(left_list)
    return (
        points,
        jnp.asarray(derivative, jnp.float32),
        jnp.asarray(end_right / quad_weights, jnp.float32),
        jnp.asarray(end_left / quad_weights, jnp.float32),
        jnp.asarray(end_right, jnp.float32),
        jnp.asarray(end_left, jnp.float32),
    )


def speed_grid(point_count):
    return -SPEED_LIMIT + (np.arange(point_count) + 0.5) * (2.0 * SPEED_LIMIT / point_count)


def shift_velocity(field_entries, offset, keep_mask):
    padding = jnp.zeros(field_entries.shape[:-1] + (abs(offset),), field_entries.dtype)
    if offset > 0:
        shifted = jnp.concatenate([field_entries[..., offset:], padding], -1)
    else:
        shifted = jnp.concatenate([padding, field_entries[..., :offset]], -1)
    return jnp.where(keep_mask, shifted, 0.0)


def on_device(distribution, z_order, edge_codes):
    local_r, local_z, vdev = distribution.shape
    row_count = local_r // NODES
    col_count = local_z // NODES
    node_count = local_r * local_z
    plane_size = NVR * NVT
    slot_count = vdev // plane_size
    row_index = lax.axis_index("row")
    gz_index = lax.axis_index("gz")
    row_total = lax.axis_size("row")
    gz_total = lax.axis_size("gz")
    points, derivative, lift_right, lift_left, end_right, end_left = dg_tables(NODES)
    weight = (
        2
        * SPEED_LIMIT
        / NVR
        * (2 * SPEED_LIMIT / NVT)
        * (2 * SPEED_LIMIT / NVZ)
        / (2 * math.pi) ** 1.5
    )
    grid_r = speed_grid(NVR)
    grid_t = speed_grid(NVT)
    grid_z = speed_grid(NVZ)
    half_flux = float(
        weight
        * np.sum(np.exp(-(grid_r**2) / 2))
        * np.sum(np.exp(-(grid_t**2) / 2))
        * np.sum(np.maximum(grid_z, 0.0) * np.exp(-(grid_z**2) / 2))
    )
    vel_r = jnp.tile(jnp.asarray(np.repeat(grid_r, NVT), jnp.float32), slot_count)
    vel_t = jnp.tile(jnp.asarray(np.tile(grid_t, NVR), jnp.float32), slot_count)
    slot_speeds = jnp.sum(
        jnp.where(
            z_order[:, None] == jnp.arange(NVZ, dtype=jnp.int32)[None, :],
            jnp.asarray(grid_z, jnp.float32)[None, :],
            0.0,
        ),
        1,
    )
    vel_z = jnp.repeat(slot_speeds, plane_size)
    flat_index = jnp.arange(vdev, dtype=jnp.int32)
    a_index = flat_index // NVT % NVR
    b_index = flat_index % NVT
    speed_sq = vel_r**2 + vel_t**2 + vel_z**2
    maxwell_wall = jnp.exp(-speed_sq / 2)
    element_start = (row_index * row_count).astype(jnp.float32)
    radius = (
        (element_start + jnp.arange(row_count, dtype=jnp.float32))[:, None]
        + (1.0 + jnp.asarray(points, jnp.float32))[None, :] / 2
    ) * ELEMENT_WIDTH
    radius = radius.reshape(local_r)
    code_bottom = jnp.repeat(edge_codes[0], NODES)
    code_top = jnp.repeat(edge_codes[1], NODES)
    down_coef = weight * jnp.maximum(-vel_z, 0.0)
    up_coef = weight * jnp.maximum(vel_z, 0.0)

    def gather_moments(current):
        bottom = jnp.einsum("j,rjv->rv", end_left, current[:, :NODES], precision=HIGHEST_PRECISION)
        top_trace = jnp.einsum(
            "j,rjv->rv", end_right, current[:, local_z - NODES :], precision=HIGHEST_PRECISION
        )
        edge_trace = jnp.where(gz_index == 0, bottom, top_trace)
        first_coef = jnp.where(gz_index == 0, down_coef, up_coef)
        bound_sums = jnp.stack(
            [
                jnp.dot(edge_trace, first_coef, precision=HIGHEST_PRECISION),
                jnp.dot(edge_trace, down_coef, precision=HIGHEST_PRECISION),
            ]
        )
        flat = current.reshape(node_count, vdev)
        moment_basis = jnp.stack(
            [
                jnp.full((vdev,), weight, jnp.float32),
                weight * vel_r,
                weight * vel_t,
                weight * vel_z,
                0.5 * weight * speed_sq,
            ],
            1,
        )
        partials = jnp.dot(
            flat, moment_basis, precision=HIGHEST_PRECISION, preferred_element_type=jnp.float32
        )
        integral_sums_table, bound_sums = lax.psum((partials, bound_sums), "vert")
        particle_concentration = integral_sums_table[:, 0]
        bulk_velocity = integral_sums_table[:, 1:4] / particle_concentration[:, None]
        vapour_warmth = (
            2.0 * integral_sums_table[:, 4] / particle_concentration - jnp.sum(bulk_velocity**2, 1)
        ) / 3.0
        thermal_norm_square = (
            (vel_r[None, :] - bulk_velocity[:, 0:1]) ** 2
            + (vel_t[None, :] - bulk_velocity[:, 1:2]) ** 2
            + (vel_z[None, :] - bulk_velocity[:, 2:3]) ** 2
        )
        weighted = flat * thermal_norm_square
        heat_basis = jnp.stack(
            [
                weight * vel_r,
                weight * vel_t,
                weight * vel_z,
                jnp.full((vdev,), weight, jnp.float32),
            ],
            1,
        )
        heat_parts = jnp.dot(
            weighted, heat_basis, precision=HIGHEST_PRECISION, preferred_element_type=jnp.float32
        )
        heat_local = 0.5 * (heat_parts[:, :3] - bulk_velocity * heat_parts[:, 3:4])
        conduction_integral = lax.psum(heat_local, "vert")
        fluid_observables = (
            particle_concentration,
            bulk_velocity[:, 0],
            bulk_velocity[:, 1],
            bulk_velocity[:, 2],
            vapour_warmth,
            conduction_integral[:, 0],
            conduction_integral[:, 1],
            conduction_integral[:, 2],
        )
        fluid_observables = tuple((entry.reshape(local_r, local_z) for entry in fluid_observables))
        return (fluid_observables, bound_sums)

    def advance(current, fluid_observables, bound_sums):
        (
            particle_concentration,
            drift_outward,
            drift_around,
            drift_lengthwise,
            vapour_warmth,
            conduction_outward,
            conduction_around,
            conduction_lengthwise,
        ) = tuple((entry[:, :, None] for entry in fluid_observables))
        grouped = current.reshape(row_count, NODES, local_z, vdev)
        volume = jnp.einsum("ij,ejzv->eizv", derivative, grouped, precision=HIGHEST_PRECISION)
        trace_hi = jnp.einsum("j,ejzv->ezv", end_right, grouped, precision=HIGHEST_PRECISION)
        trace_lo = jnp.einsum("j,ejzv->ezv", end_left, grouped, precision=HIGHEST_PRECISION)
        mirror = (
            trace_lo[0].reshape(local_z, slot_count, NVR, NVT)[:, :, ::-1, :].reshape(local_z, vdev)
        )
        edge_halo = with_halo(jnp.stack([trace_lo[0], trace_hi[-1]]), (("row", 0),), 1)
        from_left = edge_halo[0]
        from_right = edge_halo[3]
        left_ghost = jnp.where(row_index == 0, mirror, from_left)
        right_ghost = jnp.where(row_index == row_total - 1, trace_hi[-1], from_right)
        plus_side = jnp.concatenate([left_ghost[None], trace_hi], 0)
        minus_side = jnp.concatenate([trace_lo, right_ghost[None]], 0)
        face_values = jnp.where(vel_r > 0, plus_side, minus_side)
        radial = (
            2.0
            / ELEMENT_WIDTH
            * vel_r
            * (
                volume
                + lift_right[None, :, None, None] * (face_values[1:] - trace_hi)[:, None]
                - lift_left[None, :, None, None] * (face_values[:-1] - trace_lo)[:, None]
            )
        )
        radial = radial.reshape(local_r, local_z, vdev)
        grouped = current.reshape(local_r, col_count, NODES, vdev)
        volume = jnp.einsum("ij,rejv->reiv", derivative, grouped, precision=HIGHEST_PRECISION)
        trace_hi = jnp.einsum("j,rejv->rev", end_right, grouped, precision=HIGHEST_PRECISION)
        trace_lo = jnp.einsum("j,rejv->rev", end_left, grouped, precision=HIGHEST_PRECISION)
        edge_halo = with_halo(jnp.stack([trace_lo[:, 0], trace_hi[:, -1]]), (("gz", 0),), 1)
        bottom_density = jnp.where(code_bottom == 1, SAT_DENSITY, bound_sums[0] / half_flux)
        top_density = bound_sums[0] / half_flux
        bottom_ghost = bottom_density[:, None] * maxwell_wall[None, :]
        top_ghost = jnp.where(
            code_top[:, None] == 2, trace_hi[:, -1], top_density[:, None] * maxwell_wall[None, :]
        )
        low_ghost = jnp.where(gz_index == 0, bottom_ghost, edge_halo[0])
        high_ghost = jnp.where(gz_index == gz_total - 1, top_ghost, edge_halo[3])
        plus_side = jnp.concatenate([low_ghost[:, None], trace_hi], 1)
        minus_side = jnp.concatenate([trace_lo, high_ghost[:, None]], 1)
        face_values = jnp.where(vel_z > 0, plus_side, minus_side)
        axial_term = (
            2.0
            / ELEMENT_WIDTH
            * vel_z
            * (
                volume
                + lift_right[None, None, :, None] * (face_values[:, 1:] - trace_hi)[:, :, None]
                - lift_left[None, None, :, None] * (face_values[:, :-1] - trace_lo)[:, :, None]
            )
        )
        axial_term = axial_term.reshape(local_r, local_z, vdev)
        step_r = 2 * SPEED_LIMIT / NVR
        step_t = 2 * SPEED_LIMIT / NVT
        grad_r = (
            shift_velocity(current, NVT, a_index < NVR - 1)
            - shift_velocity(current, -NVT, a_index > 0)
        ) / (2 * step_r)
        grad_t = (
            shift_velocity(current, 1, b_index < NVT - 1) - shift_velocity(current, -1, b_index > 0)
        ) / (2 * step_t)
        rotation = (vel_t * vel_t * grad_r - vel_r * vel_t * grad_t) / radius[:, None, None]
        peculiar_r = vel_r - drift_outward
        peculiar_t = vel_t - drift_around
        peculiar_z = vel_z - drift_lengthwise
        thermal_norm_square = peculiar_r**2 + peculiar_t**2 + peculiar_z**2
        projected_conduction = (
            peculiar_r * conduction_outward
            + peculiar_t * conduction_around
            + peculiar_z * conduction_lengthwise
        )
        gaussian_resting_state = (
            particle_concentration
            * vapour_warmth ** (-1.5)
            * jnp.exp(-thermal_norm_square / (2 * vapour_warmth))
        )
        collision_goal_state = gaussian_resting_state * (
            1.0
            + (1.0 - VISCOUS_RATIO)
            * projected_conduction
            / (5.0 * particle_concentration * vapour_warmth**2)
            * (thermal_norm_square / vapour_warmth - 5.0)
        )
        collide = particle_concentration / KNUDSEN * (collision_goal_state - current)
        return current + TIME_STEP * (collide - radial - axial_term - rotation)

    current = distribution
    for step_index in range(STEPS):
        fluid_observables, bound_sums = gather_moments(current)
        current = advance(current, fluid_observables, bound_sums)
    fluid_observables, bound_sums = gather_moments(current)
    macroscopic = jnp.stack(fluid_observables)
    bottom_row = jnp.where(code_bottom == 1, SAT_DENSITY * half_flux - bound_sums[0], 0.0)
    top_row = jnp.where(code_top == 2, bound_sums[0] - bound_sums[1], 0.0)
    boundary_flux = jnp.where(gz_index == 0, bottom_row, top_row)[None]
    return (current, macroscopic, boundary_flux)


def solution(mesh):
    in_specs = (P("row", "gz", "vert"), P("vert"), P(None, "row"))
    out_specs = (P("row", "gz", "vert"), P(None, "row", "gz"), P("gz", "row"))
    return jax.shard_map(
        on_device, mesh=mesh, in_specs=in_specs, out_specs=out_specs, check_vma=False
    )
```

profile of v0, /device:TPU:1, one launch (start us, length us, event | category | flops | bytes accessed | tf_op | source)
XLA Modules:
  0.0 535.6 jit_solution(1569821555901534045)
XLA Ops:
  0.7 5.3 fusion.58
  7.1 1.4 collective-permute-start.3
  8.5 5.0 fusion.150
  15.1 1.5 collective-permute-start.1
  17.8 2.2 fusion.114
  20.1 2.2 fusion.112
  22.3 5.5 %fusion.148 = f32[1,16,6912]{2,0,1:T(1,128)} fusion(f32[8,1,1]{0,1,2:T(1,128)S(1)} %copy-done.53, f32[8,16,6912]{2,1,0:T(8,128)S(1)} %copy-done), kind=kOutput, calls=%fused_computation.303 | convolution fusion | flops 10616832 | bytes 3981344 | tf_op jit(solution)/shard_map/j,ejzv->ezv/dot_general | solution.py:267
  27.8 4.1 fusion.158
  31.9 4.1 fusion.157
  38.0 1.4 sub.385
  41.5 1.4 sub.375
  45.0 1.4 sub.380
  51.7 1.7 stack.24
  53.4 4.4 convolution_bitcast_fusion.4
  57.8 36.2 %psum.63 = f32[128,5]{0,1:T(8,128)} all-reduce(f32[128,5]{0,1:T(8,128)} %convolution_bitcast_fusion.4), channel_id=1, replica_groups=mesh['row'=4,'gz'=2,'vert'=16] {'vert'}, use_global_device_ids=true, to_apply=%region_1.2 | all-reduce | flops 640 | bytes 5120 | tf_op jit(solution)/shard_map/psum | solution.py:215
  97.1 4.7 fusion.83
  123.6 1.5 multiply_multiply_fusion
  125.1 1.6 fusion.132
  126.8 1.6 fusion.133
  129.0 38.5 %all-reduce.10 = (f32[2,8]{1,0:T(2,128)}, f32[128,3]{0,1:T(4,128)}) all-reduce(f32[2,8]{1,0:T(2,128)} %pad_maximum_fusion.1, f32[128,3]{0,1:T(4,128)} %subtract_multiply_fusion.14), channel_id=1, replica_groups=mesh['row'=4,'gz'=2,'vert'=16] {'vert'}, use_global_device_ids=true, to_apply=%region_4.5 | all-reduce | flops 400 | bytes 3200 | tf_op jit(solution)/shard_map/psum | solution.py:215
  179.8 3.8 fusion.60
  185.4 2.8 reshape_squeeze.6
  188.3 3.5 rev.6
  191.8 2.5 reshape.690
  194.3 4.2 copy.204
  198.5 2.1 copy.203
  200.6 2.1 copy.206
  202.7 3.8 copy.205
  207.3 1.4 broadcast_select_fusion.3
  208.8 4.2 collective-permute-start.2
  214.1 4.2 collective-permute-start
  219.9 3.7 fusion.5
  223.7 3.8 copy.96
  230.0 14.4 %fusion.23 = f32[8,16,6912]{2,0,1:T(8,128)S(1)} fusion(f32[8,16,6912]{2,0,1:T(8,128)} %bitcast.312, f32[8,8,1]{1,0,2:T(8,128)S(1)} %copy-done.105, f32[8,16,6911]{2,0,1:T(8,128)S(1)} %copy.203, f32[8,16,6911]{2,0,1:T(8,128)S(1)} %copy.204, f32[8,16,6864]{2,0,1:T(8,128)} %copy.205, f32[8,16,6864]{2,0,1:T(8,128)S(1)} %copy.206, f32[8]{0:T(128)S(1)} %add_multiply_fusion, ...), kind=kOutput, calls=%fused_computation.27 | convolution fusion | flops 124747776 | bytes 25806688 | tf_op jit(solution)/shard_map/ij,ejzv->eizv/dot_general | solution.py:266
  244.5 4.0 fusion.95
  248.5 4.0 fusion.93
  252.5 4.3 fusion.164
  256.8 3.1 fusion.163
  259.9 2.9 copy.102
  263.1 2.0 fusion.104
  265.1 2.0 fusion.102
  269.4 4.1 fusion.154
  273.5 4.0 fusion.155
  279.3 1.5 collective-permute-start.7
  283.1 2.8 reshape_squeeze.7
  285.9 3.1 rev.7
  289.0 2.5 reshape.695
  291.5 5.4 %fusion.162 = f32[128,5]{0,1:T(8,128)} fusion(f32[128,6912]{1,0:T(8,128)} %bitcast.309, f32[6912,5]{0,1:T(8,128)} %stack.24), kind=kOutput, calls=%fused_computation.317 | convolution fusion | flops 53084160 | bytes 3679744 | tf_op jit(solution)/shard_map/dot_general | solution.py:212
  296.9 34.4 %psum.66 = f32[128,5]{0,1:T(8,128)} all-reduce(f32[128,5]{0,1:T(8,128)} %fusion.162), channel_id=1, replica_groups=mesh['row'=4,'gz'=2,'vert'=16] {'vert'}, use_global_device_ids=true, to_apply=%region_5.6 | all-reduce | flops 640 | bytes 5120 | tf_op jit(solution)/shard_map/psum | solution.py:215
  334.6 5.9 %fusion.73 = f32[128,4]{0,1:T(4,128)S(1)} fusion(f32[128,6912]{1,0:T(8,128)} %bitcast.310, f32[128]{0:T(128)S(1)} %get-tuple-element.110, f32[128]{0:T(128)S(1)} %get-tuple-element.109, f32[128]{0:T(128)S(1)} %get-tuple-element.108, f32[6912]{0:T(1024)} %sub.385, f32[6912]{0:T(1024)} %sub.380, f32[6912]{0:T(1024)} %sub.375, f32[6912,1]{0,1:T(1,128)} %broadcast.609, ...), kind=kOutput, calls=%fused_computation.89 | convolution fusion | flops 50512896 | bytes 3736064 | tf_op jit(solution)/shard_map/dot_general | solution.py:236
  363.5 33.9 %all-reduce.9 = (f32[2,8]{1,0:T(2,128)}, f32[128,3]{0,1:T(4,128)}) all-reduce(f32[2,8]{1,0:T(2,128)} %pad_maximum_fusion.2, f32[128,3]{0,1:T(4,128)} %subtract_multiply_fusion.13), channel_id=1, replica_groups=mesh['row'=4,'gz'=2,'vert'=16] {'vert'}, use_global_device_ids=true, to_apply=%region_8.9 | all-reduce | flops 400 | bytes 3200 | tf_op jit(solution)/shard_map/psum | solution.py:215
  408.6 1.5 broadcast_select_fusion.2
  410.1 5.1 collective-permute-start.6
  416.5 4.5 collective-permute-start.4
  422.0 1.9 maximum_select_fusion.3
  424.5 4.8 fusion.2
  429.3 3.8 copy.115
  435.9 11.2 %fusion.18 = f32[8,16,6912]{2,0,1:T(8,128)S(1)} fusion(f32[8,16,6912]{2,0,1:T(8,128)S(1)} %fusion.23, f32[8,16,6912]{2,0,1:T(8,128)} %bitcast.311, f32[8,8,1]{1,0,2:T(8,128)S(1)} %copy-done.106, f32[8,16,6911]{2,0,1:T(8,128)} %get-tuple-element.57, f32[8,16,6911]{2,0,1:T(8,128)S(1)} %copy-done.22, f32[8,16,6864]{2,0,1:T(8,128)S(1)} %copy-done.21, ...), kind=kOutput, calls=%fused_computation.22 | convolution fusion | flops 124747776 | bytes 25806688 | tf_op jit(solution)/shard_map/ij,ejzv->eizv/dot_general | solution.py:266
  448.9 2.0 fusion.100
  451.0 2.0 fusion.98
  454.2 2.8 fusion.165
  457.1 34.0 %psum.69 = f32[128,5]{0,1:T(8,128)S(1)} all-reduce(f32[128,5]{0,1:T(8,128)S(1)} %fusion.165), channel_id=1, replica_groups=mesh['row'=4,'gz'=2,'vert'=16] {'vert'}, use_global_device_ids=true, to_apply=%region_9.10 | all-reduce | flops 640 | bytes 5120 | tf_op jit(solution)/shard_map/psum | solution.py:215
  492.8 4.7 fusion.63
  500.5 33.2 %all-reduce.8 = (f32[128,3]{0,1:T(4,128)S(1)}, f32[2,8]{1,0:T(2,128)S(1)}) all-reduce(f32[128,3]{0,1:T(4,128)S(1)} %subtract_multiply_fusion.12, f32[2,8]{1,0:T(2,128)S(1)} %pad_maximum_fusion.3), channel_id=1, replica_groups=mesh['row'=4,'gz'=2,'vert'=16] {'vert'}, use_global_device_ids=true, to_apply=%region_11.12 | all-reduce | flops 400 | bytes 3200 | tf_op jit(solution)/shard_map/psum | solution.py:240
  (359 shorter events, 117.9 us)
Async XLA Ops:
  0.6 7.9 %copy-start.56 = (f32[8,1,1]{0,1,2:T(1,128)S(1)}, f32[8,1,1]{0,1,2:T(1,128)}, u32[]{:S(2)}) copy-start(f32[8,1,1]{0,1,2:T(1,128)} %constant.164) | copy-start | bytes 100
  0.6 7.9 %copy-start = (f32[8,16,6912]{2,1,0:T(8,128)S(1)}, f32[8,16,6912]{2,1,0:T(8,128)}, u32[]{:S(2)}) copy-start(f32[8,16,6912]{2,1,0:T(8,128)} %param.12) | copy-start | bytes 10616836
  7.1 13.0 %copy-start.53 = (f32[8,1,1]{0,1,2:T(1,128)S(1)}, f32[8,1,1]{0,1,2:T(1,128)}, u32[]{:S(2)}) copy-start(f32[8,1,1]{0,1,2:T(1,128)} %constant.165) | copy-start | bytes 100
  7.1 200.2 %collective-permute-start.3 = (f32[1,8,6912]{2,0,1:T(1,128)}, f32[1,8,6912]{2,0,1:T(1,128)}, u32[]{:S(2)}, u32[]{:S(2)}) collective-permute-start(f32[1,8,6912]{2,0,1:T(1,128)} %slice_bitcast_fusion.1), channel_id=1, source_target_pairs={{16,0},{17,1},{18,2},{19,3},{20,4},{21,5},{22,6},{23,7},{24,8},{25... | collective-permute-start | bytes 663560 | tf_op jit(solution)/shard_map/ppermute | solution.py:35
  15.1 197.9 %collective-permute-start.1 = (f32[1,16,6912]{2,1,0:T(8,128)}, f32[1,16,6912]{2,1,0:T(8,128)}, u32[]{:S(2)}, u32[]{:S(2)}) collective-permute-start(f32[1,16,6912]{2,1,0:T(8,128)} %copy.216), channel_id=1, source_target_pairs={{32,0},{64,32},{96,64},{33,1},{65,33},{97,65},{34,2},{66,34},{98,6... | collective-permute-start | bytes 1327112 | tf_op jit(solution)/shard_map/ppermute | solution.py:35
  31.9 4.1 copy-start.100
  31.9 4.1 copy-start.104
  31.9 4.8 copy-start.96
  125.1 3.3 copy-start.34
  194.3 4.2 copy-start.4
  202.7 4.6 copy-start.103
  202.7 4.7 copy-start.27
  202.7 4.7 copy-start.30
  202.7 4.7 copy-start.98
  202.7 10.3 %copy-start.18 = (f32[1,16,6912]{2,0,1:T(1,128)S(1)}, f32[1,16,6912]{2,0,1:T(1,128)}, u32[]{:S(2)}) copy-start(f32[1,16,6912]{2,0,1:T(1,128)} %fusion.148) | copy-start | bytes 1327108
  202.7 15.6 %copy-start.97 = (f32[8]{0:T(128)S(1)}, f32[8]{0:T(128)}, u32[]{:S(2)}) copy-start(f32[8]{0:T(128)} %broadcast_select_fusion.14) | copy-start | bytes 100
  202.7 15.8 %copy-start.25 = (f32[1,8,2,6912]{3,2,1,0:T(2,128)S(1)}, f32[1,8,2,6912]{3,2,1,0:T(2,128)}, u32[]{:S(2)}) copy-start(f32[1,8,2,6912]{3,2,1,0:T(2,128)} %copy-done.24) | copy-start | bytes 1327108
  206.5 12.7 %copy-start.9 = (f32[1,8,2,6912]{3,0,2,1:T(1,128)S(1)}, f32[1,8,2,6912]{3,0,2,1:T(1,128)}, u32[]{:S(2)}) copy-start(f32[1,8,2,6912]{3,0,2,1:T(1,128)} %copy-done.8) | copy-start | bytes 1327108
  206.5 12.8 %copy-start.17 = (f32[1,8,2,6912]{3,0,2,1:T(1,128)S(1)}, f32[1,8,2,6912]{3,0,2,1:T(1,128)}, u32[]{:S(2)}) copy-start(f32[1,8,2,6912]{3,0,2,1:T(1,128)} %copy-done.16) | copy-start | bytes 1327108
  207.3 21.9 %copy-start.101 = (f32[8]{0:T(128)}, f32[8]{0:T(128)S(1)}, u32[]{:S(2)}) copy-start(f32[8]{0:T(128)S(1)} %add_multiply_fusion) | copy-start | bytes 100
  208.7 11.2 %copy-start.37 = (f32[6912]{0:T(1024)S(1)}, f32[6912]{0:T(1024)}, u32[]{:S(2)}) copy-start(f32[6912]{0:T(1024)} %get-tuple-element.86) | copy-start | bytes 82948
  208.7 11.2 %copy-start.51 = (f32[8,8,1,1]{1,0,3,2:T(8,128)S(1)}, f32[8,8,1,1]{1,0,3,2:T(8,128)}, u32[]{:S(2)}) copy-start(f32[8,8,1,1]{1,0,3,2:T(8,128)} %constant.166) | copy-start | bytes 772
  208.7 11.2 %copy-start.89 = (f32[8]{0:T(128)S(1)}, f32[8]{0:T(128)}, u32[]{:S(2)}) copy-start(f32[8]{0:T(128)} %constant.131.clone) | copy-start | bytes 100
  208.8 11.2 %copy-start.91 = (f32[8]{0:T(128)S(1)}, f32[8]{0:T(128)}, u32[]{:S(2)}) copy-start(f32[8]{0:T(128)} %constant.130.clone) | copy-start | bytes 100
  208.8 9.5 %collective-permute-start.2 = (f32[1,8,6912]{2,0,1:T(1,128)S(1)}, f32[1,8,6912]{2,0,1:T(1,128)S(1)}, u32[]{:S(2)}, u32[]{:S(2)}) collective-permute-start(f32[1,8,6912]{2,0,1:T(1,128)S(1)} %get-tuple-element.83), channel_id=1, source_target_pairs={{0,16},{1,17},{2,18},{3,19},{4,20},{5,21},{6,22},{7,23},{8,24},{9,... | collective-permute-start | bytes 663560 | tf_op jit(solution)/shard_map/ppermute | solution.py:33
  214.1 13.7 %collective-permute-start = (f32[1,16,6912]{2,1,0:T(8,128)S(1)}, f32[1,16,6912]{2,1,0:T(8,128)S(1)}, u32[]{:S(2)}, u32[]{:S(2)}) collective-permute-start(f32[1,16,6912]{2,1,0:T(8,128)S(1)} %get-tuple-element.79), channel_id=1, source_target_pairs={{0,32},{32,64},{64,96},{1,33},{33,65},{65,97},{2,34},{34,66},{66,9... | collective-permute-start | bytes 1327112 | tf_op jit(solution)/shard_map/ppermute | solution.py:33
  223.7 4.1 copy-start.29
  230.0 14.5 %copy-start.94 = (f32[8,1,1,1]{0,1,3,2:T(1,128)S(1)}, f32[8,1,1,1]{0,1,3,2:T(1,128)}, u32[]{:S(2)}) copy-start(f32[8,1,1,1]{0,1,3,2:T(1,128)} %constant.167) | copy-start | bytes 100
  244.5 4.0 copy-start.93
  244.5 8.0 %copy-start.54 = (f32[8,1,1]{0,1,2:T(1,128)S(1)}, f32[8,1,1]{0,1,2:T(1,128)}, u32[]{:S(2)}) copy-start(f32[8,1,1]{0,1,2:T(1,128)} %constant.165) | copy-start | bytes 100
  248.5 32.3 %copy-start.12 = (f32[1,8,2,6912]{3,0,2,1:T(1,128)}, f32[1,8,2,6912]{3,0,2,1:T(1,128)S(1)}, u32[]{:S(2)}) copy-start(f32[1,8,2,6912]{3,0,2,1:T(1,128)S(1)} %fusion.95) | copy-start | bytes 1327108
  248.5 8.3 %copy-start.57 = (f32[8,1,1]{0,1,2:T(1,128)S(1)}, f32[8,1,1]{0,1,2:T(1,128)}, u32[]{:S(2)}) copy-start(f32[8,1,1]{0,1,2:T(1,128)} %constant.164) | copy-start | bytes 100
  252.5 25.7 %copy-start.14 = (f32[1,8,2,6912]{3,0,2,1:T(1,128)}, f32[1,8,2,6912]{3,0,2,1:T(1,128)S(1)}, u32[]{:S(2)}) copy-start(f32[1,8,2,6912]{3,0,2,1:T(1,128)S(1)} %fusion.93) | copy-start | bytes 1327108
  259.9 17.5 %copy-start.10 = (f32[1,16,6912]{2,0,1:T(1,128)}, f32[1,16,6912]{2,0,1:T(1,128)S(1)}, u32[]{:S(2)}) copy-start(f32[1,16,6912]{2,0,1:T(1,128)S(1)} %fusion.163) | copy-start | bytes 1327108
  263.0 4.1 copy-start.35
  263.1 5.2 copy-start.32
  278.5 3.3 copy-start.26
  279.3 129.3 %collective-permute-start.7 = (f32[1,8,6912]{2,0,1:T(1,128)}, f32[1,8,6912]{2,0,1:T(1,128)}, u32[]{:S(2)}, u32[]{:S(2)}) collective-permute-start(f32[1,8,6912]{2,0,1:T(1,128)} %slice_bitcast_fusion), channel_id=1, source_target_pairs={{16,0},{17,1},{18,2},{19,3},{20,4},{21,5},{22,6},{23,7},{24,8},{25... | collective-permute-start | bytes 663560 | tf_op jit(solution)/shard_map/ppermute | solution.py:35
  281.8 133.4 %collective-permute-start.5 = (f32[1,16,6912]{2,1,0:T(8,128)}, f32[1,16,6912]{2,1,0:T(8,128)}, u32[]{:S(2)}, u32[]{:S(2)}) collective-permute-start(f32[1,16,6912]{2,1,0:T(8,128)} %copy.215), channel_id=1, source_target_pairs={{32,0},{64,32},{96,64},{33,1},{65,33},{97,65},{34,2},{66,34},{98,6... | collective-permute-start | bytes 1327112 | tf_op jit(solution)/shard_map/ppermute | solution.py:35
  407.8 16.1 %copy-start.13 = (f32[1,8,2,6912]{3,0,2,1:T(1,128)S(1)}, f32[1,8,2,6912]{3,0,2,1:T(1,128)}, u32[]{:S(2)}) copy-start(f32[1,8,2,6912]{3,0,2,1:T(1,128)} %copy-done.12) | copy-start | bytes 1327108
  407.8 16.1 %copy-start.15 = (f32[1,8,2,6912]{3,0,2,1:T(1,128)S(1)}, f32[1,8,2,6912]{3,0,2,1:T(1,128)}, u32[]{:S(2)}) copy-start(f32[1,8,2,6912]{3,0,2,1:T(1,128)} %copy-done.14) | copy-start | bytes 1327108
  410.1 14.4 %copy-start.38 = (f32[6912]{0:T(1024)S(1)}, f32[6912]{0:T(1024)}, u32[]{:S(2)}) copy-start(f32[6912]{0:T(1024)} %get-tuple-element.86) | copy-start | bytes 82948
  410.1 14.4 %copy-start.52 = (f32[8,8,1,1]{1,0,3,2:T(8,128)S(1)}, f32[8,8,1,1]{1,0,3,2:T(8,128)}, u32[]{:S(2)}) copy-start(f32[8,8,1,1]{1,0,3,2:T(8,128)} %constant.166) | copy-start | bytes 772
  410.1 14.4 %copy-start.90 = (f32[8]{0:T(128)S(1)}, f32[8]{0:T(128)}, u32[]{:S(2)}) copy-start(f32[8]{0:T(128)} %constant.131.clone) | copy-start | bytes 100
  410.1 14.4 %copy-start.92 = (f32[8]{0:T(128)S(1)}, f32[8]{0:T(128)}, u32[]{:S(2)}) copy-start(f32[8]{0:T(128)} %constant.130.clone) | copy-start | bytes 100
  410.1 10.8 %collective-permute-start.6 = (f32[1,8,6912]{2,0,1:T(1,128)S(1)}, f32[1,8,6912]{2,0,1:T(1,128)S(1)}, u32[]{:S(2)}, u32[]{:S(2)}) collective-permute-start(f32[1,8,6912]{2,0,1:T(1,128)S(1)} %get-tuple-element.77), channel_id=1, source_target_pairs={{0,16},{1,17},{2,18},{3,19},{4,20},{5,21},{6,22},{7,23},{8,24},{9,... | collective-permute-start | bytes 663560 | tf_op jit(solution)/shard_map/ppermute | solution.py:33
  416.5 17.0 %collective-permute-start.4 = (f32[1,16,6912]{2,1,0:T(8,128)S(1)}, f32[1,16,6912]{2,1,0:T(8,128)S(1)}, u32[]{:S(2)}, u32[]{:S(2)}) collective-permute-start(f32[1,16,6912]{2,1,0:T(8,128)S(1)} %get-tuple-element.73), channel_id=1, source_target_pairs={{0,32},{32,64},{64,96},{1,33},{33,65},{65,97},{2,34},{34,66},{66,9... | collective-permute-start | bytes 1327112 | tf_op jit(solution)/shard_map/ppermute | solution.py:33
  424.5 8.9 %copy-start.28 = (f32[1,16,6912]{2,1,0:T(8,128)S(1)}, f32[1,16,6912]{2,1,0:T(8,128)}, u32[]{:S(2)}) copy-start(f32[1,16,6912]{2,1,0:T(8,128)} %reshape.695) | copy-start | bytes 1327108
  429.3 6.4 %copy-start.21 = (f32[8,16,6864]{2,0,1:T(8,128)S(1)}, f32[8,16,6864]{2,0,1:T(8,128)}, u32[]{:S(2)}) copy-start(f32[8,16,6864]{2,0,1:T(8,128)} %get-tuple-element.55) | copy-start | bytes 10543108
  429.3 6.4 %copy-start.22 = (f32[8,16,6911]{2,0,1:T(8,128)S(1)}, f32[8,16,6911]{2,0,1:T(8,128)}, u32[]{:S(2)}) copy-start(f32[8,16,6911]{2,0,1:T(8,128)} %get-tuple-element.56) | copy-start | bytes 10615300
  433.2 2.5 copy-start.20
  433.2 2.5 copy-start.40
  433.2 2.5 copy-start.42
  433.2 2.5 copy-start.44
  433.2 2.5 copy-start.46
  433.2 2.5 copy-start.48
  433.2 2.5 copy-start.50
  433.2 2.5 copy-start.64
  448.2 44.5 %copy-start.5 = (f32[8,16,6912]{2,1,0:T(8,128)}, f32[8,16,6912]{2,1,0:T(8,128)S(1)}, u32[]{:S(2)}) copy-start(f32[8,16,6912]{2,1,0:T(8,128)S(1)} %copy.117) | copy-start | bytes 10616836
  448.3 2.7 copy-start.55
  448.5 4.5 copy-start.36
  448.5 5.1 copy-start.33
  448.5 5.7 %copy-start.23 = (f32[6912,5]{0,1:T(8,128)S(1)}, f32[6912,5]{0,1:T(8,128)}, u32[]{:S(2)}) copy-start(f32[6912,5]{0,1:T(8,128)} %stack.24) | copy-start | bytes 414724
  492.8 4.7 copy-start.95
  (51 other events, 107.5 us)
where the time goes:
time: 547 us; the launch traced here: 536 us
  blocking collectives  210 us (38%)
  local copies, waits for them, and re-layouts  142 us (26%)
  matrix products  116 us (21%)
  other arithmetic  39.1 us (7%)
  starting transfers between devices  23.6 us (4%)
    psum x5, blocking collectives, gather_moments(): integral_sums_table, bound_sums = lax.psum((partials, bound_sums), 'vert')  177 us
    psum x1, blocking collectives, gather_moments(): conduction_integral = lax.psum(heat_local, 'vert')  33.2 us
    dot_general x2, matrix products, advance(): jnp.einsum('ij,ejzv->eizv', derivative, grouped, precision=HIGHEST_PRECIS...  25.6 us
    unnamed x231, local copies, waits for them, and re-layouts  20.8 us
    ppermute x4, starting transfers between devices, with_halo(): lax.ppermute(tail, axis, [(i, (i + 1) % count) for i in range(ends)])  18 us
    slice x4, local copies, waits for them, and re-layouts, shift_velocity(): shifted = jnp.concatenate([field_entries[..., offset:], padding], -1)  16.2 us
    dot_general x3, matrix products, gather_moments(): jnp.dot(weighted, heat_basis, precision=HIGHEST_PRECISION, preferred_elem...  15.2 us
    dot_general x3, matrix products, gather_moments(): jnp.dot(flat, moment_basis, precision=HIGHEST_PRECISION, preferred_elemen...  12.6 us
  transfers between devices with their start and end apart: 8, of which 0 were waited for; matrix products, arithmetic and copies ran while one was open for 38% of the time, Pallas kernels for 0%

commit v1 on v0

v1 whole, which is shorter than its diff:
```python
import functools
import math

import jax
import jax.numpy as jnp
import ml_dtypes
import numpy as np
from jax import lax
from jax.experimental import pallas as pl
from jax.experimental.pallas import tpu as pltpu
from jax.sharding import PartitionSpec as P

NODES = 8
NVR = 48
NVT = 48
NVZ = 48
STEPS = 2

ELEMENT_WIDTH = 4.0
TIME_STEP = 0.001
KNUDSEN = 0.005
VISCOUS_RATIO = 2.0 / 3.0
SAT_DENSITY = 1.5
SPEED_LIMIT = 5.0

PLANE = NVR * NVT
HALF = PLANE // 2
GRID_STEP = 2 * SPEED_LIMIT / NVR
UNIT = GRID_STEP / 2
MESH_IDS = pl.DeviceIdType.MESH
F32 = jnp.float32
BF16 = jnp.bfloat16


def legendre_pair(position, point_count):
    previous = 1.0
    current = position
    for degree in range(2, point_count + 1):
        previous, current = (
            current,
            ((2 * degree - 1) * position * current - (degree - 1) * previous) / degree,
        )
    slope = point_count * (position * current - previous) / (position * position - 1.0)
    return (current, slope)


def dg_tables(point_count):
    point_list = []
    weight_list = []
    for number in range(point_count):
        position = math.cos(math.pi * (number + 0.75) / (point_count + 0.5))
        for sweep in range(60):
            value, slope = legendre_pair(position, point_count)
            position = position - value / slope
        value, slope = legendre_pair(position, point_count)
        point_list.append(position)
        weight_list.append(2.0 / ((1.0 - position * position) * slope * slope))
    point_list = point_list[::-1]
    weight_list = weight_list[::-1]
    products = []
    for row_number in range(point_count):
        product_value = 1.0
        for other in range(point_count):
            if other != row_number:
                product_value = product_value * (point_list[row_number] - point_list[other])
        products.append(product_value)
    derivative_rows = []
    for row_number in range(point_count):
        entries = []
        for column in range(point_count):
            if column == row_number:
                total_value = 0.0
                for other in range(point_count):
                    if other != row_number:
                        total_value = total_value + 1.0 / (
                            point_list[row_number] - point_list[other]
                        )
                entries.append(total_value)
            else:
                entries.append(
                    products[row_number]
                    / products[column]
                    / (point_list[row_number] - point_list[column])
                )
        derivative_rows.append(entries)
    right_list = []
    left_list = []
    for column in range(point_count):
        right_value = 1.0
        left_value = 1.0
        for other in range(point_count):
            if other != column:
                right_value = right_value * (1.0 - point_list[other])
                left_value = left_value * (-1.0 - point_list[other])
        right_list.append(right_value / products[column])
        left_list.append(left_value / products[column])
    points = np.array(point_list)
    quad_weights = np.array(weight_list)
    derivative = np.array(derivative_rows)
    end_right = np.array(right_list)
    end_left = np.array(left_list)
    return (
        points,
        derivative,
        end_right / quad_weights,
        end_left / quad_weights,
        end_right,
        end_left,
    )


def speed_grid(point_count):
    return -SPEED_LIMIT + (np.arange(point_count) + 0.5) * (2.0 * SPEED_LIMIT / point_count)


def split_exact(values, count):
    parts = []
    rest = np.asarray(values, np.float64)
    for _ in range(count):
        head = rest.astype(ml_dtypes.bfloat16).astype(np.float64)
        parts.append(head)
        rest = rest - head
    assert not np.any(rest)
    return parts


def constants():
    points, derivative, lift_right, lift_left, end_right, end_left = dg_tables(NODES)
    eye8, eye16 = np.eye(8), np.eye(16)
    scale = -TIME_STEP * 2.0 / ELEMENT_WIDTH
    plus = derivative + np.outer(lift_left, end_left)
    minus = derivative - np.outer(lift_right, end_right)
    radial = np.zeros((3, 128, 160))
    for k, (core, ghost) in enumerate(
        [(minus, lift_right), (derivative, 0 * lift_right), (plus, -lift_left)]
    ):
        radial[k, :, :128] = np.kron(core, eye16)
        radial[k, :, 128:144] = np.kron(ghost[:, None], eye16)
    up = np.zeros((16, 16))
    up[:8, :8] = plus
    up[8:, 8:] = plus
    up[8:, :8] = -np.outer(lift_left, end_right)
    down = np.zeros((16, 16))
    down[:8, :8] = minus
    down[8:, 8:] = minus
    down[:8, 8:] = np.outer(lift_right, end_left)
    outflow = down.copy()
    outflow[8:, 8:] = derivative
    none = np.zeros(16)
    up_ghost = np.concatenate([-lift_left, np.zeros(8)])
    down_ghost = np.concatenate([np.zeros(8), lift_right])
    axial = np.zeros((5, 128, 160))
    for k, (core, ghost) in enumerate(
        [(up, none), (up, up_ghost), (down, down_ghost), (down, none), (outflow, none)]
    ):
        axial[k, :, :128] = np.kron(eye8, core)
        axial[k, :, 144:152] = np.kron(eye8, ghost[:, None])
    low_first = np.concatenate([end_left, np.zeros(8)])
    high_last = np.concatenate([np.zeros(8), end_right])
    trace = np.zeros((2, 2, 32, 128))
    for g, across in enumerate([high_last, low_first]):
        for h, along in enumerate([end_left, end_right]):
            trace[g, h, :16] = np.kron(along[None, :], eye16)
            trace[g, h, 16:24] = np.kron(eye8, across[None, :])
    odd = 2.0 * np.arange(48) + 1 - 48
    nr, nt = np.repeat(odd, 48), np.tile(odd, 48)
    square = nr * nr + nt * nt
    columns = (
        [np.ones(PLANE), nr, nt]
        + split_exact(nr * nr, 2)
        + split_exact(nt * nt, 2)
        + split_exact(nr * nt, 2)
        + split_exact(nr * square, 3)
        + split_exact(nt * square, 3)
        + [np.zeros(PLANE)]
    )
    basis = np.stack(columns)
    grid = speed_grid(48)
    vr, vt = np.repeat(grid, 48), np.tile(grid, 48)
    a, b = np.repeat(np.arange(48), 48), np.tile(np.arange(48), 48)
    turn_r = -TIME_STEP * vt * vt / (2 * GRID_STEP)
    turn_t = TIME_STEP * vr * vt / (2 * GRID_STEP)
    rows = np.stack(
        [
            vr,
            vt,
            np.exp(-(vr**2 + vt**2) / 2),
            turn_r * (a < 47),
            -turn_r * (a > 0),
            turn_t * (b < 47),
            -turn_t * (b > 0),
            0 * vr,
        ]
    )
    ones8 = np.ones(8)
    edge = np.zeros((128, 384))
    edge[:, :128] = np.kron(eye8, np.outer(low_first, np.ones(16)))
    edge[:, 128:256] = np.kron(eye8, np.outer(high_last, np.ones(16)))
    edge[:, 256:264] = np.kron(eye8, low_first[:, None])
    edge[:, 264:272] = np.kron(eye8, high_last[:, None])
    wall = np.zeros((8, 128))
    wall[0] = np.kron(ones8, np.concatenate([-scale * lift_left, np.zeros(8)]))
    wall[1] = np.kron(ones8, np.concatenate([np.zeros(8), scale * lift_right]))
    weight = GRID_STEP**3 / (2 * math.pi) ** 1.5
    half_flux = (
        weight
        * np.sum(np.exp(-(grid**2) / 2)) ** 2
        * np.sum(np.maximum(grid, 0.0) * np.exp(-(grid**2) / 2))
    )
    as_bf16 = lambda x: jnp.asarray(x.astype(np.float32).astype(ml_dtypes.bfloat16))
    as_f32 = lambda x: jnp.asarray(x.astype(np.float32))
    arrays = (
        as_bf16(scale * radial),
        as_f32(scale * axial),
        as_bf16(trace),
        as_bf16(basis),
        as_f32(rows),
        as_f32(edge),
        as_f32(wall),
    )
    return arrays, float(weight), float(half_flux), [float(x) for x in points]


def kernel(
    sizes, weight, half_flux, points,
    f_hbm, order, codes, radial_hbm, axial_hbm, trace_hbm, basis_hbm, rows_hbm, edge_hbm, wall_hbm,
    out_hbm, macro, flux,
    F, X, LO, PART, TOUT, LHS, EX, PP, SM, PR, PT,
    radial, axial, trace, basis, rows, edge, wall,
    trR, trA, ghR, ghA, mine, ARB,
    load_sem, const_sem, out_sem,
    rs_send, rs_recv, as_send, as_recv, ar_send, ar_recv,
):
    row_total, vert_total = sizes
    row, gz, vert = lax.axis_index("row"), lax.axis_index("gz"), lax.axis_index("vert")
    last_row = row_total - 1

    barrier = pltpu.get_barrier_semaphore()

    def hello(k, carry):
        peer = lax.rem(vert + k, vert_total)
        pl.semaphore_signal(barrier, inc=1, device_id=(row, gz, peer), device_id_type=MESH_IDS)
        return carry

    lax.fori_loop(1, vert_total, hello, 0)
    pl.semaphore_signal(barrier, inc=1, device_id=(row, 1 - gz, vert), device_id_type=MESH_IDS)

    @pl.when(row > 0)
    def _():
        pl.semaphore_signal(barrier, inc=1, device_id=(row - 1, gz, vert), device_id_type=MESH_IDS)

    @pl.when(row < last_row)
    def _():
        pl.semaphore_signal(barrier, inc=1, device_id=(row + 1, gz, vert), device_id_type=MESH_IDS)

    loads = [
        pltpu.make_async_copy(f_hbm.at[:, pl.ds(s * PLANE, PLANE)], F.at[s], load_sem.at[s])
        for s in range(3)
    ]
    consts = [
        pltpu.make_async_copy(src, dst, const_sem.at[k])
        for k, (src, dst) in enumerate(
            [
                (trace_hbm, trace),
                (basis_hbm, basis),
                (rows_hbm, rows),
                (radial_hbm, radial),
                (axial_hbm, axial),
                (edge_hbm, edge),
                (wall_hbm, wall),
            ]
        )
    ]
    loads[0].start()
    for copy in consts[:2]:
        copy.start()
    for copy in loads[1:]:
        copy.start()
    for copy in consts[2:]:
        copy.start()

    speeds = [(2 * order[s] - (NVZ - 1)).astype(F32) * UNIT for s in range(3)]
    bottom_code, top_code = codes[0, 0], codes[1, 0]
    zero16 = jnp.zeros((16, HALF), F32)

    def radial_copy(n, s, h):
        step = 1 if h else -1
        return pltpu.make_async_remote_copy(
            src_ref=trR.at[n, s, h],
            dst_ref=ghR.at[n, s, h],
            send_sem=rs_send.at[n, s, h],
            recv_sem=rs_recv.at[n, s, h],
            device_id=(row + step, gz, vert),
            device_id_type=MESH_IDS,
        )

    def axial_copy(n, s):
        return pltpu.make_async_remote_copy(
            src_ref=trA.at[n, s],
            dst_ref=ghA.at[n, s],
            send_sem=as_send.at[n, s],
            recv_sem=as_recv.at[n, s],
            device_id=(row, 1 - gz, vert),
            device_id_type=MESH_IDS,
        )

    def sum_copy(n, slot, peer, k):
        return pltpu.make_async_remote_copy(
            src_ref=mine.at[n],
            dst_ref=ARB.at[n, slot],
            send_sem=ar_send.at[n, k],
            recv_sem=ar_recv.at[n, slot],
            device_id=(row, gz, peer),
            device_id_type=MESH_IDS,
        )

    def send_halo(n, s):
        @pl.when(row > 0)
        def _():
            radial_copy(n, s, 0).start()

        @pl.when(row < last_row)
        def _():
            radial_copy(n, s, 1).start()

        axial_copy(n, s).start()

    def traces(n, s):
        for h in range(2):
            lanes = pl.ds(h * HALF, HALF)
            both = jnp.dot(trace[gz, h], X[s, 0:128, lanes], preferred_element_type=F32)
            trR[n, s, h] = both[0:16]
            trA[n, s, :, lanes] = both[16:24]

    def missing_ghosts(n, s):
        @pl.when(row == 0)
        def _():
            low = trR[n, s, 0]
            ghR[n, s, 1] = jnp.concatenate(
                [low[:, k * NVT : (k + 1) * NVT] for k in reversed(range(NVR // 2))], axis=1
            )

        @pl.when(row == last_row)
        def _():
            ghR[n, s, 0] = zero16

    def plane_sums(s):
        dims = (((1,), (1,)), ((), ()))
        table = lax.dot_general(basis[...], X[s, 0:128], dims, preferred_element_type=F32)
        table += lax.dot_general(basis[...], LO[s], dims, preferred_element_type=F32)
        z = speeds[s]
        g = [table[i : i + 1] for i in range(15)]
        b0, br, bt = g[0], UNIT * g[1], UNIT * g[2]
        brr, btt, brt = (UNIT**2 * (g[i] + g[i + 1]) for i in (3, 5, 7))
        br3, bt3 = (UNIT**3 * (g[i] + (g[i + 1] + g[i + 2])) for i in (9, 12))
        return [
            b0,
            br,
            bt,
            jnp.maximum(z, 0.0) * b0,
            jnp.maximum(-z, 0.0) * b0,
            brr,
            btt,
            z * z * b0,
            brt,
            z * br,
            z * bt,
            br3 + z * z * br,
            bt3 + z * z * bt,
            z * (brr + btt) + (z * z * z) * b0,
        ]

    def send_sums(n, parts):
        total = [parts[0][i] + (parts[1][i] + parts[2][i]) for i in range(14)]
        for i in range(14):
            mine[n, i : i + 1] = total[i]
        mine[n, 14:16] = jnp.zeros((2, 128), F32)
        ARB[n, vert] = mine[n]

        def send(k, carry):
            sum_copy(n, vert, lax.rem(vert + k, vert_total), k).start()
            return carry

        lax.fori_loop(1, vert_total, send, 0)

    def wait_sums(n):
        def wait(k, carry):
            source = lax.rem(vert + k, vert_total)
            sum_copy(n, source, source, k).wait_recv()
            return carry

        lax.fori_loop(1, vert_total, wait, 0)
        terms = [ARB[n, k] for k in range(vert_total)]
        while len(terms) > 1:
            terms = [terms[i] + terms[i + 1] for i in range(0, len(terms), 2)]
        return terms[0]

    def observables(S):
        m = [S[i : i + 1] for i in range(14)]
        inv = 1.0 / m[0]
        u = [m[1] * inv, m[2] * inv, (m[3] - m[4]) * inv]
        usq = u[0] * u[0] + u[1] * u[1] + u[2] * u[2]
        tr = m[5] + m[6] + m[7]
        temp = (tr * inv - usq) / 3.0
        tensor = [[m[5], m[8], m[9]], [m[8], m[6], m[10]], [m[9], m[10], m[7]]]
        heat = []
        for i in range(3):
            mixed = tensor[i][0] * u[0] + tensor[i][1] * u[1] + tensor[i][2] * u[2]
            raw = m[11 + i] - 2.0 * mixed - u[i] * tr + (2.0 * usq * m[0]) * u[i]
            heat.append((0.5 * weight) * raw)
        return weight * m[0], u, temp, heat

    def params(S):
        density, u, temp, heat = observables(S)
        edges = jnp.dot(S, edge[:, 0:256], preferred_element_type=F32, precision=lax.Precision.HIGHEST)
        incident = weight * edges[4:5, 0:128]
        upward = weight * edges[3:4, 128:256]
        bottom = jnp.where(bottom_code == 1, SAT_DENSITY, incident / half_flux)
        top = jnp.where(top_code == 2, 0.0, upward / half_flux)
        wall_gain = jnp.where(gz == 0, bottom * wall[0:1], top * wall[1:2])
        inv_temp = 1.0 / temp
        kappa = ((1.0 - VISCOUS_RATIO) / 5.0) * inv_temp * inv_temp / density
        rate = (TIME_STEP / KNUDSEN) * density
        peak = rate * density * inv_temp * lax.rsqrt(temp)
        out = [u[0], u[1], inv_temp, kappa * heat[0], kappa * heat[1], 1.0 - rate]
        for s in range(3):
            z = speeds[s]
            cz = z - u[2]
            inward = jnp.where(gz == 0, jnp.maximum(z, 0.0), jnp.minimum(z, 0.0))
            out += [
                kappa * heat[2] * cz,
                cz * cz * inv_temp,
                peak * jnp.exp(-0.5 * cz * cz * inv_temp),
                inward * wall_gain * jnp.exp(jnp.zeros((1, 128), F32) - 0.5 * z * z),
            ]
        for i, value in enumerate(out):
            PR[i : i + 1] = value
        PT[...] = PR[...].T

    PR[...] = jnp.zeros((128, 128), F32)
    for copy in consts[:2]:
        copy.wait()
    parts = []
    for s in range(3):
        loads[s].wait()

        def split(r, carry, s=s):
            at = pl.ds(pl.multiple_of(r * 16, 16), 16)
            x = F[s, at, :]
            hi = x.astype(BF16)
            X[s, at, :] = hi
            LO[s, at, :] = (x - hi.astype(F32)).astype(BF16)
            return carry

        lax.fori_loop(0, 8, split, 0)
        traces(0, s)
        if s == 0:
            peers = vert_total + (row > 0).astype(jnp.int32) + (row < last_row).astype(jnp.int32)
            pl.semaphore_wait(barrier, peers)

        send_halo(0, s)
        parts.append(plane_sums(s))
    send_sums(0, parts)

    for copy in consts[2:]:
        copy.wait()
    for s in range(3):
        z = speeds[s]
        up = jnp.where(gz == 0, axial[0], axial[1])
        down = jnp.where(gz == 0, axial[2], jnp.where(top_code == 2, axial[4], axial[3]))
        along = (z * jnp.where(z > 0, up, down)).astype(BF16)
        for h in range(2):
            LHS[s, h, 128:256] = along
        LHS[s, 0, 0:128] = radial[jnp.where(row == last_row, 1, 0)]
        LHS[s, 1, 0:128] = radial[2]

    first = row.astype(F32)

    for n in range(STEPS):
        def rotate(r, carry):
            at = pl.ds(pl.multiple_of(r * 16, 16), 16)
            place = 0.0
            for i in range(NODES):
                place = jnp.where(r == i, (1.0 + points[i]) / 2, place)
            scale = 1.0 / ((first + place) * ELEMENT_WIDTH + jnp.zeros((16, 128), F32))
            scale = scale[:, 0:1]
            for s in range(3):
                x = F[s, at, :]
                turn = (
                    rows[3:4] * pltpu.roll(x, PLANE - NVT, 1)
                    + rows[4:5] * pltpu.roll(x, NVT, 1)
                    + rows[5:6] * pltpu.roll(x, PLANE - 1, 1)
                    + rows[6:7] * pltpu.roll(x, 1, 1)
                )
                PART[s, at, :] = turn * scale
            return carry

        lax.fori_loop(0, 8, rotate, 0)

        for s in range(3):
            missing_ghosts(n, s)

            @pl.when(row < last_row)
            def _():
                radial_copy(n, s, 0).wait_recv()

            @pl.when(row > 0)
            def _():
                radial_copy(n, s, 1).wait_recv()

            axial_copy(n, s).wait_recv()
            X[s, 144:160, :] = jnp.concatenate(
                [ghA[n, s], jnp.zeros((8, PLANE), F32)], axis=0
            ).astype(BF16)
            for h in range(2):
                lanes = pl.ds(h * HALF, HALF)
                X[s, 128:144, lanes] = ghR[n, s, h].astype(BF16)
                TOUT[s, :, lanes] = jnp.dot(
                    LHS[s, h], X[s, :, lanes], preferred_element_type=F32
                )

        params(wait_sums(n))

        def plane(r, carry):
            at = pl.ds(pl.multiple_of(r * 16, 16), 16)
            cr = rows[0:1] - PT[at, 0:1]
            ct = rows[1:2] - PT[at, 1:2]
            inv_temp = PT[at, 2:3]
            square = cr * cr + ct * ct
            EX[at, :] = jnp.exp(square * (-0.5 * inv_temp))
            SM[at, :] = square * inv_temp - 5.0
            PP[at, :] = cr * PT[at, 3:4] + ct * PT[at, 4:5]
            return carry

        lax.fori_loop(0, 8, plane, 0)

        parts = []
        for s in range(3):

            def update(r, carry, s=s):
                at = pl.ds(pl.multiple_of(r * 16, 16), 16)
                below = pl.ds(pl.multiple_of(r * 16 + 128, 16), 16)
                keep = PT[at, 5:6]
                a_s, b_s, c_s, w_s = (PT[at, 6 + 4 * s + i : 7 + 4 * s + i] for i in range(4))
                for j in range(6):
                    lanes = pl.ds(j * 384, 384)
                    goal = (EX[at, lanes] * c_s) * (
                        1.0 + (PP[at, lanes] + a_s) * (SM[at, lanes] + b_s)
                    )
                    x = (
                        keep * F[s, at, lanes]
                        + PART[s, at, lanes]
                        + rows[0:1, lanes] * TOUT[s, at, lanes]
                        + TOUT[s, below, lanes]
                        + w_s * rows[2:3, lanes]
                        + goal
                    )
                    F[s, at, lanes] = x
                    hi = x.astype(BF16)
                    X[s, at, lanes] = hi
                    LO[s, at, lanes] = (x - hi.astype(F32)).astype(BF16)
                return carry

            lax.fori_loop(0, 8, update, 0)
            if n + 1 < STEPS:
                traces(n + 1, s)
                send_halo(n + 1, s)
            else:
                pltpu.make_async_copy(
                    F.at[s], out_hbm.at[:, pl.ds(s * PLANE, PLANE)], out_sem.at[s]
                ).start()
            parts.append(plane_sums(s))
        send_sums(n + 1, parts)

    S = wait_sums(STEPS)
    density, u, temp, heat = observables(S)
    for i, value in enumerate([density] + u + [temp] + heat):
        PR[i : i + 1] = value
    final = PR[0:8]
    for r in range(8):
        macro[:, r, :] = final[:, r * 16 : (r + 1) * 16]
    edges = weight * jnp.dot(
        S, edge[:, 256:384], preferred_element_type=F32, precision=lax.Precision.HIGHEST
    )
    incident, upward, downward = edges[4:5, 0:8], edges[3:4, 8:16], edges[4:5, 8:16]
    flux[...] = jnp.where(
        gz == 0,
        jnp.where(bottom_code == 1, SAT_DENSITY * half_flux - incident, 0.0),
        jnp.where(top_code == 2, upward - downward, 0.0),
    )

    for s in range(3):
        pltpu.make_async_copy(
            F.at[s], out_hbm.at[:, pl.ds(s * PLANE, PLANE)], out_sem.at[s]
        ).wait()
    for n in range(STEPS):
        for s in range(3):

            @pl.when(row > 0)
            def _():
                radial_copy(n, s, 0).wait_send()

            @pl.when(row < last_row)
            def _():
                radial_copy(n, s, 1).wait_send()

            axial_copy(n, s).wait_send()
    for n in range(STEPS + 1):

        def done(k, carry, n=n):
            sum_copy(n, vert, lax.rem(vert + k, vert_total), k).wait_send()
            return carry

        lax.fori_loop(1, vert_total, done, 0)


def solution(mesh):
    row_total, vert_total = mesh.shape["row"], mesh.shape["vert"]
    arrays, weight, half_flux, points = constants()

    def on_device(distribution, z_order, edge_codes):
        f = distribution.reshape(128, 3 * PLANE)
        hbm = pl.BlockSpec(memory_space=pl.ANY)
        smem = pl.BlockSpec(memory_space=pltpu.SMEM)
        vmem = pl.BlockSpec(memory_space=pltpu.VMEM)
        dma = pltpu.SemaphoreType.DMA
        new, macro, flux = pl.pallas_call(
            functools.partial(kernel, (row_total, vert_total), weight, half_flux, points),
            out_shape=(
                jax.ShapeDtypeStruct((128, 3 * PLANE), F32),
                jax.ShapeDtypeStruct((8, 8, 16), F32),
                jax.ShapeDtypeStruct((1, 8), F32),
            ),
            in_specs=[hbm, smem, smem] + [hbm] * len(arrays),
            out_specs=(hbm, vmem, vmem),
            scratch_shapes=[
                pltpu.VMEM((3, 128, PLANE), F32),
                pltpu.VMEM((3, 160, PLANE), BF16),
                pltpu.VMEM((3, 128, PLANE), BF16),
                pltpu.VMEM((3, 128, PLANE), F32),
                pltpu.VMEM((3, 256, PLANE), F32),
                pltpu.VMEM((3, 2, 256, 160), BF16),
                pltpu.VMEM((128, PLANE), F32),
                pltpu.VMEM((128, PLANE), F32),
                pltpu.VMEM((128, PLANE), F32),
                pltpu.VMEM((128, 128), F32),
                pltpu.VMEM((128, 128), F32),
            ]
            + [pltpu.VMEM(x.shape, x.dtype) for x in arrays]
            + [
                pltpu.VMEM((STEPS, 3, 2, 16, HALF), F32),
                pltpu.VMEM((STEPS, 3, 8, PLANE), F32),
                pltpu.VMEM((STEPS, 3, 2, 16, HALF), F32),
                pltpu.VMEM((STEPS, 3, 8, PLANE), F32),
                pltpu.VMEM((STEPS + 1, 16, 128), F32),
                pltpu.VMEM((STEPS + 1, vert_total, 16, 128), F32),
                dma((3,)),
                dma((len(arrays),)),
                dma((3,)),
                dma((STEPS, 3, 2)),
                dma((STEPS, 3, 2)),
                dma((STEPS, 3)),
                dma((STEPS, 3)),
                dma((STEPS + 1, vert_total)),
                dma((STEPS + 1, vert_total)),
            ],
            compiler_params=pltpu.CompilerParams(
                collective_id=0, has_side_effects=True, vmem_limit_bytes=56 * 1024 * 1024
            ),
        )(f, z_order, edge_codes, *arrays)
        return new.reshape(distribution.shape), macro, flux

    in_specs = (P("row", "gz", "vert"), P("vert"), P(None, "row"))
    out_specs = (P("row", "gz", "vert"), P(None, "row", "gz"), P("gz", "row"))
    return jax.shard_map(
        on_device, mesh=mesh, in_specs=in_specs, out_specs=out_specs, check_vma=False
    )
```

time: 547 us -> 55.7 us (0.10); the launches traced: 536 us -> 55.6 us
  blocking collectives: 210 us -> 0 us
  local copies, waits for them, and re-layouts: 142 us -> 6.48 us
  matrix products: 116 us -> 0 us
  Pallas kernels: 0 us -> 48.4 us
  other arithmetic: 39.1 us -> 0 us
  starting transfers between devices: 23.6 us -> 0 us
    psum x6 -> x0, blocking collectives: 210 us -> none  [the longest x5 177 us: gather_moments(): integral_sums_table, bound_sums = lax.psum((partials, bound_sums), 'vert')]
    dot_general x30 -> x0, matrix products: 116 us -> none  [the longest x2 25.6 us: advance(): jnp.einsum('ij,ejzv->eizv', derivative, grouped, precision=HIGHEST_PRECIS...]
    pallas_call x0 -> x1, Pallas kernels: none -> 48.4 us  [on_device(): pl.pallas_call(functools.partial(kernel, (row_total, vert_total), weight,...]
    mul x27 -> x0, local copies, waits for them, and re-layouts: 34.3 us -> none  [the longest x2 7.69 us: advance(): 2.0 / ELEMENT_WIDTH * vel_z]
    ppermute x8 -> x0, starting transfers between devices: 23.6 us -> none  [the longest x4 18 us: with_halo(): lax.ppermute(tail, axis, [(i, (i + 1) % count) for i in range(ends)])]
    slice x12 -> x0, local copies, waits for them, and re-layouts: 21.2 us -> none  [the longest x4 16.2 us: shift_velocity(): shifted = jnp.concatenate([field_entries[..., offset:], padding], -1)]
    sub x16 -> x0, local copies, waits for them, and re-layouts: 20.7 us -> none  [the longest x5 6.72 us: advance(): peculiar_r = vel_r - drift_outward]
    another operation x18 -> x0, local copies, waits for them, and re-layouts: 17.4 us -> none  [the longest x2 5.61 us: advance(): trace_lo[0].reshape(local_z, slot_count, NVR, NVT)[:, :, ::-1, :]]
  transfers between devices with their start and end apart: 8 -> 0, of which waited for: 0 -> 0; matrix products, arithmetic and copies ran while one was open for 38% -> 0% of each run, Pallas kernels for 0% -> 0%
where the time goes in v1:
time: 55.7 us; the launch traced here: 55.6 us
  Pallas kernels  48.4 us (87%)
  local copies, waits for them, and re-layouts  6.48 us (12%)
  between operations  0.66 us (1%)
    pallas_call x1, Pallas kernels, on_device(): pl.pallas_call(functools.partial(kernel, (row_total, vert_total), weight,...  48.4 us
    unnamed x8, local copies, waits for them, and re-layouts  6.48 us

profile of v1, /device:TPU:1, one launch (start us, length us, event | category | flops | bytes accessed | tf_op | source)
XLA Modules:
  0.0 55.6 jit_solution(11567409978392113738)
XLA Ops:
  0.6 1.3 %copy.13.codes = s32[2,1]{1,0:T(2,128)} copy(s32[2,1]{0,1:T(1,128)} %param.12) | data formatting | bytes 16 | tf_op args[2]
  1.9 48.4 %shard_map.121 = (f32[128,6912]{1,0:T(8,128)}, f32[8,8,16]{2,1,0:T(8,128)}, f32[1,8]{1,0:T(1,128)}) custom-call(f32[128,6912]{1,0:T(8,128)} %bitcast.2, s32[3]{0:T(128)} %order.1, s32[2,1]{1,0:T(2,128)} %copy.13.codes, bf16[3,128,160]{2,1,0:T(8,128)(2,1)} %constant.14.clone.radial_hbm, f32[5,128,160]{2,1,0:T(8,128)} %constant.15.clone.axial_hbm, ...), custom_call_target="tpu_custom_call" | custom-call | tf_op jit(solution)/shard_map/pallas_call | solution.py:627
  50.4 0.0 copy-start
  50.4 0.0 copy-start.1
  50.4 4.0 %copy.17 = f32[8,16,6912]{2,1,0:T(8,128)} copy(f32[8,16,6912]{2,1,0:T(8,128)} %bitcast.3) | data formatting | bytes 7077888
  54.4 0.0 copy-done
  54.4 0.6 %copy.18 = f32[8,8,16]{2,1,0:T(8,128)} copy(f32[8,8,16]{2,1,0:T(8,128)S(1)} %copy-done) | data formatting | bytes 8192
  55.1 0.0 copy-done.1
  55.1 0.5 copy.19
Async XLA Ops:
  50.4 4.1 %copy-start = (f32[8,8,16]{2,1,0:T(8,128)S(1)}, f32[8,8,16]{2,1,0:T(8,128)}, u32[]{:S(2)}) copy-start(f32[8,8,16]{2,1,0:T(8,128)} %get-tuple-element.13) | copy-start | bytes 12292
  50.4 4.7 %copy-start.1 = (f32[1,8]{1,0:T(1,128)S(1)}, f32[1,8]{1,0:T(1,128)}, u32[]{:S(2)}) copy-start(f32[1,8]{1,0:T(1,128)} %get-tuple-element.14) | copy-start | bytes 100

commit v2 on v1

--- a/solution.py
+++ b/solution.py
@@ -176,20 +176,16 @@
     )
     basis = np.stack(columns)
     grid = speed_grid(48)
-    vr, vt = np.repeat(grid, 48), np.tile(grid, 48)
-    a, b = np.repeat(np.arange(48), 48), np.tile(np.arange(48), 48)
-    turn_r = -TIME_STEP * vt * vt / (2 * GRID_STEP)
-    turn_t = TIME_STEP * vr * vt / (2 * GRID_STEP)
+    column = np.ones((1, 128))
+    index = np.arange(48)
+    turn = TIME_STEP * grid / (2 * GRID_STEP)
     rows = np.stack(
         [
-            vr,
-            vt,
-            np.exp(-(vr**2 + vt**2) / 2),
-            turn_r * (a < 47),
-            -turn_r * (a > 0),
-            turn_t * (b < 47),
-            -turn_t * (b > 0),
-            0 * vr,
+            grid[:, None] * column,
+            np.exp(-(grid**2) / 2)[:, None] * column,
+            (-turn * grid)[:, None] * column,
+            (turn * (index < 47))[:, None] * column,
+            (turn * (index > 0))[:, None] * column,
         ]
     )
     ones8 = np.ones(8)
@@ -201,6 +197,7 @@
     wall = np.zeros((8, 128))
     wall[0] = np.kron(ones8, np.concatenate([-scale * lift_left, np.zeros(8)]))
     wall[1] = np.kron(ones8, np.concatenate([np.zeros(8), scale * lift_right]))
+    wall[2] = np.kron((1.0 + np.array(points)) / 2, np.ones(16))
     weight = GRID_STEP**3 / (2 * math.pi) ** 1.5
     half_flux = (
         weight
@@ -210,25 +207,25 @@
     as_bf16 = lambda x: jnp.asarray(x.astype(np.float32).astype(ml_dtypes.bfloat16))
     as_f32 = lambda x: jnp.asarray(x.astype(np.float32))
     arrays = (
-        as_bf16(scale * radial),
-        as_f32(scale * axial),
+        as_bf16(scale * radial.transpose(0, 2, 1)),
+        as_f32(scale * axial.transpose(0, 2, 1)),
         as_bf16(trace),
         as_bf16(basis),
         as_f32(rows),
         as_f32(edge),
         as_f32(wall),
     )
-    return arrays, float(weight), float(half_flux), [float(x) for x in points]
+    return arrays, float(weight), float(half_flux)
 
 
 def kernel(
-    sizes, weight, half_flux, points,
+    sizes, weight, half_flux,
     f_hbm, order, codes, radial_hbm, axial_hbm, trace_hbm, basis_hbm, rows_hbm, edge_hbm, wall_hbm,
-    out_hbm, macro, flux,
-    F, X, LO, PART, TOUT, LHS, EX, PP, SM, PR, PT,
+    out, macro, flux,
+    RAW, F, X, LO, PART, TOUT, W, TURN, BYT, BYR, PR,
     radial, axial, trace, basis, rows, edge, wall,
     trR, trA, ghR, ghA, mine, ARB,
-    load_sem, const_sem, out_sem,
+    load_sem, const_sem,
     rs_send, rs_recv, as_send, as_recv, ar_send, ar_recv,
 ):
     row_total, vert_total = sizes
@@ -254,7 +251,7 @@
         pl.semaphore_signal(barrier, inc=1, device_id=(row + 1, gz, vert), device_id_type=MESH_IDS)
 
     loads = [
-        pltpu.make_async_copy(f_hbm.at[:, pl.ds(s * PLANE, PLANE)], F.at[s], load_sem.at[s])
+        pltpu.make_async_copy(f_hbm.at[:, pl.ds(s * PLANE, PLANE)], RAW.at[s], load_sem.at[s])
         for s in range(3)
     ]
     consts = [
@@ -280,7 +277,7 @@
         copy.start()
 
     speeds = [(2 * order[s] - (NVZ - 1)).astype(F32) * UNIT for s in range(3)]
-    bottom_code, top_code = codes[0, 0], codes[1, 0]
+    bottom_code, top_code = codes[0], codes[1]
     zero16 = jnp.zeros((16, HALF), F32)
 
     def radial_copy(n, s, h):
@@ -314,6 +311,13 @@
             device_id_type=MESH_IDS,
         )
 
+    def each_peer(action):
+        def body(k, carry):
+            action(lax.rem(vert + k, vert_total), k)
+            return carry
+
+        lax.fori_loop(1, vert_total, body, 0)
+
     def send_halo(n, s):
         @pl.when(row > 0)
         def _():
@@ -325,29 +329,60 @@
 
         axial_copy(n, s).start()
 
+    over_lanes = (((1,), (1,)), ((), ()))
+
     def traces(n, s):
         for h in range(2):
-            lanes = pl.ds(h * HALF, HALF)
-            both = jnp.dot(trace[gz, h], X[s, 0:128, lanes], preferred_element_type=F32)
+            here = pl.ds(h * HALF, HALF)
+            both = lax.dot_general(
+                trace[gz, h], X[s, here, 0:128], over_lanes, preferred_element_type=F32
+            )
             trR[n, s, h] = both[0:16]
-            trA[n, s, :, lanes] = both[16:24]
-
-    def missing_ghosts(n, s):
+            trA[n, s, :, here] = both[16:24]
+
+    def ghost_columns(s, h, table):
+        for k in range(HALF // 128):
+            X[s, h * HALF + k * 128 : h * HALF + (k + 1) * 128, 128:160] = (
+                table[:, k * 128 : (k + 1) * 128].T.astype(BF16)
+            )
+
+    def ghosts(n, s):
+        @pl.when(row < last_row)
+        def _():
+            radial_copy(n, s, 0).wait_recv()
+
+        @pl.when(row > 0)
+        def _():
+            radial_copy(n, s, 1).wait_recv()
+
+        axial_copy(n, s).wait_recv()
+        spare = jnp.zeros((8, HALF), F32)
+        low = [ghA[n, s, :, 0:HALF], spare]
+        high = [ghA[n, s, :, HALF:PLANE], spare]
+
+        @pl.when(row < last_row)
+        def _():
+            ghost_columns(s, 0, jnp.concatenate([ghR[n, s, 0]] + low, axis=0))
+
+        @pl.when(row == last_row)
+        def _():
+            ghost_columns(s, 0, jnp.concatenate([zero16] + low, axis=0))
+
+        @pl.when(row > 0)
+        def _():
+            ghost_columns(s, 1, jnp.concatenate([ghR[n, s, 1]] + high, axis=0))
+
         @pl.when(row == 0)
         def _():
-            low = trR[n, s, 0]
-            ghR[n, s, 1] = jnp.concatenate(
-                [low[:, k * NVT : (k + 1) * NVT] for k in reversed(range(NVR // 2))], axis=1
+            own = trR[n, s, 0]
+            mirror = jnp.concatenate(
+                [own[:, k * NVT : (k + 1) * NVT] for k in reversed(range(NVR // 2))], axis=1
             )
-
-        @pl.when(row == last_row)
-        def _():
-            ghR[n, s, 0] = zero16
+            ghost_columns(s, 1, jnp.concatenate([mirror] + high, axis=0))
 
     def plane_sums(s):
-        dims = (((1,), (1,)), ((), ()))
-        table = lax.dot_general(basis[...], X[s, 0:128], dims, preferred_element_type=F32)
-        table += lax.dot_general(basis[...], LO[s], dims, preferred_element_type=F32)
+        table = jnp.dot(basis[...], X[s, :, 0:128], preferred_element_type=F32)
+        table += jnp.dot(basis[...], LO[s], preferred_element_type=F32)
         z = speeds[s]
         g = [table[i : i + 1] for i in range(15)]
         b0, br, bt = g[0], UNIT * g[1], UNIT * g[2]
@@ -371,32 +406,21 @@
         ]
 
     def send_sums(n, parts):
-        total = [parts[0][i] + (parts[1][i] + parts[2][i]) for i in range(14)]
         for i in range(14):
-            mine[n, i : i + 1] = total[i]
+            mine[n, i : i + 1] = parts[0][i] + (parts[1][i] + parts[2][i])
         mine[n, 14:16] = jnp.zeros((2, 128), F32)
         ARB[n, vert] = mine[n]
-
-        def send(k, carry):
-            sum_copy(n, vert, lax.rem(vert + k, vert_total), k).start()
-            return carry
-
-        lax.fori_loop(1, vert_total, send, 0)
-
-    def wait_sums(n):
-        def wait(k, carry):
-            source = lax.rem(vert + k, vert_total)
-            sum_copy(n, source, source, k).wait_recv()
-            return carry
-
-        lax.fori_loop(1, vert_total, wait, 0)
+        each_peer(lambda peer, k: sum_copy(n, vert, peer, k).start())
+
+    def wait_totals(n):
+        each_peer(lambda peer, k: sum_copy(n, peer, peer, k).wait_recv())
         terms = [ARB[n, k] for k in range(vert_total)]
         while len(terms) > 1:
             terms = [terms[i] + terms[i + 1] for i in range(0, len(terms), 2)]
-        return terms[0]
+        return [terms[0][i : i + 1] for i in range(14)]
 
     def observables(S):
-        m = [S[i : i + 1] for i in range(14)]
+        m = S
         inv = 1.0 / m[0]
         u = [m[1] * inv, m[2] * inv, (m[3] - m[4]) * inv]
         usq = u[0] * u[0] + u[1] * u[1] + u[2] * u[2]
@@ -412,9 +436,12 @@
 
     def params(S):
         density, u, temp, heat = observables(S)
-        edges = jnp.dot(S, edge[:, 0:256], preferred_element_type=F32, precision=lax.Precision.HIGHEST)
-        incident = weight * edges[4:5, 0:128]
-        upward = weight * edges[3:4, 128:256]
+        flows = jnp.concatenate([S[3], S[4], jnp.zeros((6, 128), F32)], axis=0)
+        edges = jnp.dot(
+            flows, edge[:, 0:256], preferred_element_type=F32, precision=lax.Precision.HIGHEST
+        )
+        incident = weight * edges[1:2, 0:128]
+        upward = weight * edges[0:1, 128:256]
         bottom = jnp.where(bottom_code == 1, SAT_DENSITY, incident / half_flux)
         top = jnp.where(top_code == 2, 0.0, upward / half_flux)
         wall_gain = jnp.where(gz == 0, bottom * wall[0:1], top * wall[1:2])
@@ -422,22 +449,34 @@
         kappa = ((1.0 - VISCOUS_RATIO) / 5.0) * inv_temp * inv_temp / density
         rate = (TIME_STEP / KNUDSEN) * density
         peak = rate * density * inv_temp * lax.rsqrt(temp)
-        out = [u[0], u[1], inv_temp, kappa * heat[0], kappa * heat[1], 1.0 - rate]
+        PR[0:1] = 1.0 - rate
+        centred = rows[0] - u[0]
+        square = centred * centred
+        around = [
+            jnp.exp(square * (-0.5 * inv_temp)),
+            centred * (kappa * heat[0]),
+            square * inv_temp - 5.0,
+        ]
+        centred = rows[0] - u[1]
+        square = centred * centred
+        BYT[0] = jnp.exp(square * (-0.5 * inv_temp))
+        BYT[1] = centred * (kappa * heat[1])
+        BYT[2] = square * inv_temp
         for s in range(3):
             z = speeds[s]
             cz = z - u[2]
             inward = jnp.where(gz == 0, jnp.maximum(z, 0.0), jnp.minimum(z, 0.0))
-            out += [
-                kappa * heat[2] * cz,
-                cz * cz * inv_temp,
-                peak * jnp.exp(-0.5 * cz * cz * inv_temp),
-                inward * wall_gain * jnp.exp(jnp.zeros((1, 128), F32) - 0.5 * z * z),
-            ]
-        for i, value in enumerate(out):
-            PR[i : i + 1] = value
-        PT[...] = PR[...].T
-
-    PR[...] = jnp.zeros((128, 128), F32)
+            BYR[s, 0] = around[0] * (peak * jnp.exp(-0.5 * cz * cz * inv_temp))
+            BYR[s, 1] = around[1] + kappa * heat[2] * cz
+            BYR[s, 2] = around[2] + cz * cz * inv_temp
+            BYR[s, 3] = rows[1] * (
+                inward * wall_gain * jnp.exp(jnp.zeros((1, 128), F32) - 0.5 * z * z)
+            )
+
+    for n in range(STEPS):
+        for s in range(3):
+            F[n, s, 0:NVT] = jnp.zeros((NVT, 128), F32)
+            F[n, s, NVT + PLANE :] = jnp.zeros((NVT, 128), F32)
     for copy in consts[:2]:
         copy.wait()
     parts = []
@@ -445,14 +484,15 @@
         loads[s].wait()
 
         def split(r, carry, s=s):
-            at = pl.ds(pl.multiple_of(r * 16, 16), 16)
-            x = F[s, at, :]
+            at = pl.ds(pl.multiple_of(r * 128, 128), 128)
+            x = RAW[s, :, at].T
+            F[0, s, pl.ds(pl.multiple_of(NVT + r * 128, 8), 128), :] = x
             hi = x.astype(BF16)
-            X[s, at, :] = hi
+            X[s, at, 0:128] = hi
             LO[s, at, :] = (x - hi.astype(F32)).astype(BF16)
             return carry
 
-        lax.fori_loop(0, 8, split, 0)
+        lax.fori_loop(0, PLANE // 128, split, 0, unroll=3)
         traces(0, s)
         if s == 0:
             peers = vert_total + (row > 0).astype(jnp.int32) + (row < last_row).astype(jnp.int32)
@@ -470,129 +510,88 @@
         down = jnp.where(gz == 0, axial[2], jnp.where(top_code == 2, axial[4], axial[3]))
         along = (z * jnp.where(z > 0, up, down)).astype(BF16)
         for h in range(2):
-            LHS[s, h, 128:256] = along
-        LHS[s, 0, 0:128] = radial[jnp.where(row == last_row, 1, 0)]
-        LHS[s, 1, 0:128] = radial[2]
-
-    first = row.astype(F32)
+            W[s, h, :, 128:256] = along
+        W[s, 0, :, 0:128] = radial[jnp.where(row == last_row, 1, 0)]
+        W[s, 1, :, 0:128] = radial[2]
+
+    inverse = 1.0 / ((row.astype(F32) + wall[2:3]) * ELEMENT_WIDTH)
+    for k in range(3):
+        TURN[k] = rows[2 + k] * inverse
 
     for n in range(STEPS):
-        def rotate(r, carry):
-            at = pl.ds(pl.multiple_of(r * 16, 16), 16)
-            place = 0.0
-            for i in range(NODES):
-                place = jnp.where(r == i, (1.0 + points[i]) / 2, place)
-            scale = 1.0 / ((first + place) * ELEMENT_WIDTH + jnp.zeros((16, 128), F32))
-            scale = scale[:, 0:1]
-            for s in range(3):
-                x = F[s, at, :]
-                turn = (
-                    rows[3:4] * pltpu.roll(x, PLANE - NVT, 1)
-                    + rows[4:5] * pltpu.roll(x, NVT, 1)
-                    + rows[5:6] * pltpu.roll(x, PLANE - 1, 1)
-                    + rows[6:7] * pltpu.roll(x, 1, 1)
+        for s in range(3):
+            ghosts(n, s)
+            for h in range(2):
+                here = pl.ds(h * HALF, HALF)
+                TOUT[s, here, :] = jnp.dot(X[s, here, :], W[s, h], preferred_element_type=F32)
+
+            def stream(a, carry, s=s):
+                at = pl.ds(pl.multiple_of(a * NVT, 16), NVT)
+                behind, here, ahead = (
+                    F[n, s, pl.ds(pl.multiple_of((a + k) * NVT, 8), NVT), :] for k in range(3)
                 )
-                PART[s, at, :] = turn * scale
-            return carry
-
-        lax.fori_loop(0, 8, rotate, 0)
-
-        for s in range(3):
-            missing_ghosts(n, s)
-
-            @pl.when(row < last_row)
-            def _():
-                radial_copy(n, s, 0).wait_recv()
-
-            @pl.when(row > 0)
-            def _():
-                radial_copy(n, s, 1).wait_recv()
-
-            axial_copy(n, s).wait_recv()
-            X[s, 144:160, :] = jnp.concatenate(
-                [ghA[n, s], jnp.zeros((8, PLANE), F32)], axis=0
-            ).astype(BF16)
-            for h in range(2):
-                lanes = pl.ds(h * HALF, HALF)
-                X[s, 128:144, lanes] = ghR[n, s, h].astype(BF16)
-                TOUT[s, :, lanes] = jnp.dot(
-                    LHS[s, h], X[s, :, lanes], preferred_element_type=F32
+                speed = (2 * a - (NVR - 1)).astype(F32) * UNIT
+                around = TURN[1] * pltpu.roll(here, NVT - 1, 0) - TURN[2] * pltpu.roll(here, 1, 0)
+                PART[s, at, :] = (
+                    TURN[0] * (ahead - behind)
+                    + speed * (around + TOUT[s, at, 0:128])
+                    + TOUT[s, at, 128:256]
                 )
-
-        params(wait_sums(n))
-
-        def plane(r, carry):
-            at = pl.ds(pl.multiple_of(r * 16, 16), 16)
-            cr = rows[0:1] - PT[at, 0:1]
-            ct = rows[1:2] - PT[at, 1:2]
-            inv_temp = PT[at, 2:3]
-            square = cr * cr + ct * ct
-            EX[at, :] = jnp.exp(square * (-0.5 * inv_temp))
-            SM[at, :] = square * inv_temp - 5.0
-            PP[at, :] = cr * PT[at, 3:4] + ct * PT[at, 4:5]
-            return carry
-
-        lax.fori_loop(0, 8, plane, 0)
+                return carry
+
+            lax.fori_loop(0, NVR, stream, 0, unroll=4)
+
+        params(wait_totals(n))
 
         parts = []
         for s in range(3):
 
-            def update(r, carry, s=s):
-                at = pl.ds(pl.multiple_of(r * 16, 16), 16)
-                below = pl.ds(pl.multiple_of(r * 16 + 128, 16), 16)
-                keep = PT[at, 5:6]
-                a_s, b_s, c_s, w_s = (PT[at, 6 + 4 * s + i : 7 + 4 * s + i] for i in range(4))
-                for j in range(6):
-                    lanes = pl.ds(j * 384, 384)
-                    goal = (EX[at, lanes] * c_s) * (
-                        1.0 + (PP[at, lanes] + a_s) * (SM[at, lanes] + b_s)
-                    )
-                    x = (
-                        keep * F[s, at, lanes]
-                        + PART[s, at, lanes]
-                        + rows[0:1, lanes] * TOUT[s, at, lanes]
-                        + TOUT[s, below, lanes]
-                        + w_s * rows[2:3, lanes]
-                        + goal
-                    )
-                    F[s, at, lanes] = x
-                    hi = x.astype(BF16)
-                    X[s, at, lanes] = hi
-                    LO[s, at, lanes] = (x - hi.astype(F32)).astype(BF16)
+            def update(a, carry, s=s):
+                at = pl.ds(pl.multiple_of(a * NVT, 16), NVT)
+                own = pl.ds(pl.multiple_of((a + 1) * NVT, 8), NVT)
+                peak, heat, excess, wall_row = (BYR[s, k, pl.ds(a, 1), :] for k in range(4))
+                goal = (BYT[0] * peak) * (1.0 + (BYT[1] + heat) * (BYT[2] + excess))
+                x = PR[0:1] * F[n, s, own, :] + PART[s, at, :] + wall_row * rows[1] + goal
+                F[(n + 1) % 2, s, own, :] = x
+                hi = x.astype(BF16)
+                X[s, at, 0:128] = hi
+                LO[s, at, :] = (x - hi.astype(F32)).astype(BF16)
                 return carry
 
-            lax.fori_loop(0, 8, update, 0)
+            lax.fori_loop(0, NVR, update, 0, unroll=4)
             if n + 1 < STEPS:
                 traces(n + 1, s)
                 send_halo(n + 1, s)
-            else:
-                pltpu.make_async_copy(
-                    F.at[s], out_hbm.at[:, pl.ds(s * PLANE, PLANE)], out_sem.at[s]
-                ).start()
             parts.append(plane_sums(s))
         send_sums(n + 1, parts)
 
-    S = wait_sums(STEPS)
+    for s in range(3):
+
+        def back(r, carry, s=s):
+            at = pl.ds(pl.multiple_of(r * 128, 128), 128)
+            x = F[STEPS % 2, s, pl.ds(pl.multiple_of(NVT + r * 128, 8), 128), :]
+            out[:, pl.ds(pl.multiple_of(s * PLANE + r * 128, 128), 128)] = x.T
+            return carry
+
+        lax.fori_loop(0, PLANE // 128, back, 0, unroll=3)
+    S = wait_totals(STEPS)
     density, u, temp, heat = observables(S)
     for i, value in enumerate([density] + u + [temp] + heat):
         PR[i : i + 1] = value
     final = PR[0:8]
     for r in range(8):
         macro[:, r, :] = final[:, r * 16 : (r + 1) * 16]
+    flows = jnp.concatenate([S[3], S[4], jnp.zeros((6, 128), F32)], axis=0)
     edges = weight * jnp.dot(
-        S, edge[:, 256:384], preferred_element_type=F32, precision=lax.Precision.HIGHEST
-    )
-    incident, upward, downward = edges[4:5, 0:8], edges[3:4, 8:16], edges[4:5, 8:16]
+        flows, edge[:, 256:384], preferred_element_type=F32, precision=lax.Precision.HIGHEST
+    )
+    incident, upward, downward = edges[1:2, 0:8], edges[0:1, 8:16], edges[1:2, 8:16]
     flux[...] = jnp.where(
         gz == 0,
         jnp.where(bottom_code == 1, SAT_DENSITY * half_flux - incident, 0.0),
         jnp.where(top_code == 2, upward - downward, 0.0),
     )
 
-    for s in range(3):
-        pltpu.make_async_copy(
-            F.at[s], out_hbm.at[:, pl.ds(s * PLANE, PLANE)], out_sem.at[s]
-        ).wait()
     for n in range(STEPS):
         for s in range(3):
 
@@ -606,45 +605,52 @@
 
             axial_copy(n, s).wait_send()
     for n in range(STEPS + 1):
-
-        def done(k, carry, n=n):
-            sum_copy(n, vert, lax.rem(vert + k, vert_total), k).wait_send()
-            return carry
-
-        lax.fori_loop(1, vert_total, done, 0)
+        each_peer(lambda peer, k, n=n: sum_copy(n, vert, peer, k).wait_send())
+
+
+def deliver(new, macro, flux, new_hbm, macro_hbm, flux_hbm, sems):
+    copies = [
+        pltpu.make_async_copy(src, dst, sems.at[k])
+        for k, (src, dst) in enumerate([(new, new_hbm), (macro, macro_hbm), (flux, flux_hbm)])
+    ]
+    for copy in copies:
+        copy.start()
+    for copy in copies:
+        copy.wait()
 
 
 def solution(mesh):
     row_total, vert_total = mesh.shape["row"], mesh.shape["vert"]
-    arrays, weight, half_flux, points = constants()
+    arrays, weight, half_flux = constants()
 
     def on_device(distribution, z_order, edge_codes):
         f = distribution.reshape(128, 3 * PLANE)
+        outs = (
+            jax.ShapeDtypeStruct((128, 3 * PLANE), F32),
+            jax.ShapeDtypeStruct((8, 8, 16), F32),
+            jax.ShapeDtypeStruct((1, 8), F32),
+        )
         hbm = pl.BlockSpec(memory_space=pl.ANY)
         smem = pl.BlockSpec(memory_space=pltpu.SMEM)
         vmem = pl.BlockSpec(memory_space=pltpu.VMEM)
         dma = pltpu.SemaphoreType.DMA
         new, macro, flux = pl.pallas_call(
-            functools.partial(kernel, (row_total, vert_total), weight, half_flux, points),
-            out_shape=(
-                jax.ShapeDtypeStruct((128, 3 * PLANE), F32),
-                jax.ShapeDtypeStruct((8, 8, 16), F32),
-                jax.ShapeDtypeStruct((1, 8), F32),
-            ),
+            functools.partial(kernel, (row_total, vert_total), weight, half_flux),
+            out_shape=(pltpu.VMEM(outs[0].shape, F32), outs[1], outs[2]),
             in_specs=[hbm, smem, smem] + [hbm] * len(arrays),
-            out_specs=(hbm, vmem, vmem),
+            out_specs=(vmem, vmem, vmem),
             scratch_shapes=[
                 pltpu.VMEM((3, 128, PLANE), F32),
-                pltpu.VMEM((3, 160, PLANE), BF16),
-                pltpu.VMEM((3, 128, PLANE), BF16),
-                pltpu.VMEM((3, 128, PLANE), F32),
-                pltpu.VMEM((3, 256, PLANE), F32),
-                pltpu.VMEM((3, 2, 256, 160), BF16),
-                pltpu.VMEM((128, PLANE), F32),
-                pltpu.VMEM((128, PLANE), F32),
-                pltpu.VMEM((128, PLANE), F32),
-                pltpu.VMEM((128, 128), F32),
-                pltpu.VMEM((128, 128), F32),
+                pltpu.VMEM((2, 3, PLANE + 2 * NVT, 128), F32),
+                pltpu.VMEM((3, PLANE, 160), BF16),
+                pltpu.VMEM((3, PLANE, 128), BF16),
+                pltpu.VMEM((3, PLANE, 128), F32),
+                pltpu.VMEM((3, PLANE, 256), F32),
+                pltpu.VMEM((3, 2, 160, 256), BF16),
+                pltpu.VMEM((3, NVT, 128), F32),
+                pltpu.VMEM((3, NVT, 128), F32),
+                pltpu.VMEM((3, 4, NVR, 128), F32),
+                pltpu.VMEM((8, 128), F32),
             ]
             + [pltpu.VMEM(x.shape, x.dtype) for x in arrays]
             + [
@@ -656,7 +662,6 @@
                 pltpu.VMEM((STEPS + 1, vert_total, 16, 128), F32),
                 dma((3,)),
                 dma((len(arrays),)),
-                dma((3,)),
                 dma((STEPS, 3, 2)),
                 dma((STEPS, 3, 2)),
                 dma((STEPS, 3)),
@@ -665,9 +670,17 @@
                 dma((STEPS + 1, vert_total)),
             ],
             compiler_params=pltpu.CompilerParams(
-                collective_id=0, has_side_effects=True, vmem_limit_bytes=56 * 1024 * 1024
+                collective_id=0, has_side_effects=True, vmem_limit_bytes=52 * 1024 * 1024
             ),
-        )(f, z_order, edge_codes, *arrays)
+        )(f, z_order, edge_codes.reshape(2), *arrays)
+        hold = lambda x: pltpu.with_memory_space_constraint(x, pltpu.VMEM)
+        new, macro, flux = pl.pallas_call(
+            deliver,
+            out_shape=outs,
+            in_specs=[vmem, vmem, vmem],
+            out_specs=(hbm, hbm, hbm),
+            scratch_shapes=[dma((3,))],
+        )(hold(new), macro, flux)
         return new.reshape(distribution.shape), macro, flux
 
     in_specs = (P("row", "gz", "vert"), P("vert"), P(None, "row"))

time: 55.7 us -> 42.7 us (0.77)
  Pallas kernels: 48.4 us -> 41.9 us
  local copies, waits for them, and re-layouts: 6.48 us -> 0 us
    pallas_call x1, Pallas kernels: 48.4 us -> 39.3 us  [on_device(): pl.pallas_call(functools.partial(kernel, (row_total, vert_total), weight,...]
    unnamed x8 -> x0, local copies, waits for them, and re-layouts: 6.48 us -> none
    pallas_call x0 -> x1, Pallas kernels: none -> 2.58 us  [on_device(): pl.pallas_call(deliver, out_shape=outs, in_specs=[vmem, vmem, vmem], out_...]
where the time goes in v2:
time: 42.7 us; the launch traced here: 42.5 us
  Pallas kernels  41.9 us (98%)
  between operations  0.64 us (1%)
    pallas_call x1, Pallas kernels, on_device(): pl.pallas_call(functools.partial(kernel, (row_total, vert_total), weight,...  39.3 us
    pallas_call x1, Pallas kernels, on_device(): pl.pallas_call(deliver, out_shape=outs, in_specs=[vmem, vmem, vmem], out_...  2.58 us

profile of v2, /device:TPU:1, one launch (start us, length us, event | category | flops | bytes accessed | tf_op | source)
XLA Modules:
  0.0 42.5 jit_solution(9056446291153092036)
XLA Ops:
  0.6 39.3 %shard_map.121 = (f32[128,6912]{1,0:T(8,128)S(1)}, f32[8,8,16]{2,1,0:T(8,128)}, f32[1,8]{1,0:T(1,128)}) custom-call(f32[128,6912]{1,0:T(8,128)} %bitcast.3, s32[3]{0:T(128)} %order.1, s32[2]{0:T(128)} %bitcast.4, bf16[3,160,128]{2,1,0:T(8,128)(2,1)} %constant.14.clone.radial_hbm, f32[5,160,128]{2,1,0:T(8,128)} %constant.15.clone.axial_hbm, ...), custom_call_target="tpu_custom_call" | custom-call | tf_op jit(solution)/shard_map/pallas_call | solution.py:637
  39.9 2.6 %shard_map.122 = (f32[128,6912]{1,0:T(8,128)}, f32[8,8,16]{2,1,0:T(8,128)}, f32[1,8]{1,0:T(1,128)}) custom-call(f32[128,6912]{1,0:T(8,128)S(1)} %get-tuple-element.9.new, f32[8,8,16]{2,1,0:T(8,128)} %get-tuple-element.10.macro, f32[1,8]{1,0:T(1,128)} %get-tuple-element.11.flux), custom_call_target="tpu_custom_call" | custom-call | tf_op jit(solution)/shard_map/pallas_call | solution.py:677

commit v3 on v2

--- a/solution.py
+++ b/solution.py
@@ -130,12 +130,13 @@
     scale = -TIME_STEP * 2.0 / ELEMENT_WIDTH
     plus = derivative + np.outer(lift_left, end_left)
     minus = derivative - np.outer(lift_right, end_right)
-    radial = np.zeros((3, 128, 160))
+    radial = np.zeros((3, 128, 256))
     for k, (core, ghost) in enumerate(
         [(minus, lift_right), (derivative, 0 * lift_right), (plus, -lift_left)]
     ):
         radial[k, :, :128] = np.kron(core, eye16)
-        radial[k, :, 128:144] = np.kron(ghost[:, None], eye16)
+        first = 160 if k == 2 else 128
+        radial[k, :, first : first + 16] = np.kron(ghost[:, None], eye16)
     up = np.zeros((16, 16))
     up[:8, :8] = plus
     up[8:, 8:] = plus
@@ -222,7 +223,7 @@
     sizes, weight, half_flux,
     f_hbm, order, codes, radial_hbm, axial_hbm, trace_hbm, basis_hbm, rows_hbm, edge_hbm, wall_hbm,
     out, macro, flux,
-    RAW, F, X, LO, PART, TOUT, W, TURN, BYT, BYR, PR,
+    RAW, F, G, PART, TOUT, W, TURN, BYT, BYR, PR,
     radial, axial, trace, basis, rows, edge, wall,
     trR, trA, ghR, ghA, mine, ARB,
     load_sem, const_sem,
@@ -232,28 +233,10 @@
     row, gz, vert = lax.axis_index("row"), lax.axis_index("gz"), lax.axis_index("vert")
     last_row = row_total - 1
 
-    barrier = pltpu.get_barrier_semaphore()
-
-    def hello(k, carry):
-        peer = lax.rem(vert + k, vert_total)
-        pl.semaphore_signal(barrier, inc=1, device_id=(row, gz, peer), device_id_type=MESH_IDS)
-        return carry
-
-    lax.fori_loop(1, vert_total, hello, 0)
-    pl.semaphore_signal(barrier, inc=1, device_id=(row, 1 - gz, vert), device_id_type=MESH_IDS)
-
-    @pl.when(row > 0)
-    def _():
-        pl.semaphore_signal(barrier, inc=1, device_id=(row - 1, gz, vert), device_id_type=MESH_IDS)
-
-    @pl.when(row < last_row)
-    def _():
-        pl.semaphore_signal(barrier, inc=1, device_id=(row + 1, gz, vert), device_id_type=MESH_IDS)
-
-    loads = [
-        pltpu.make_async_copy(f_hbm.at[:, pl.ds(s * PLANE, PLANE)], RAW.at[s], load_sem.at[s])
-        for s in range(3)
-    ]
+    def load(s):
+        lanes = pl.ds(pl.multiple_of(s * PLANE, 128), PLANE)
+        return pltpu.make_async_copy(f_hbm.at[:, lanes], RAW.at[s], load_sem.at[s])
+
     consts = [
         pltpu.make_async_copy(src, dst, const_sem.at[k])
         for k, (src, dst) in enumerate(
@@ -268,17 +251,47 @@
             ]
         )
     ]
-    loads[0].start()
+    load(0).start()
     for copy in consts[:2]:
         copy.start()
-    for copy in loads[1:]:
-        copy.start()
+    load(1).start()
+    load(2).start()
     for copy in consts[2:]:
         copy.start()
 
+    barrier = pltpu.get_barrier_semaphore()
+
+    def hello(k, carry):
+        peer = lax.rem(vert + k, vert_total)
+        pl.semaphore_signal(barrier, inc=1, device_id=(row, gz, peer), device_id_type=MESH_IDS)
+        return carry
+
+    lax.fori_loop(1, vert_total, hello, 0)
+    pl.semaphore_signal(barrier, inc=1, device_id=(row, 1 - gz, vert), device_id_type=MESH_IDS)
+
+    @pl.when(row > 0)
+    def _():
+        pl.semaphore_signal(barrier, inc=1, device_id=(row - 1, gz, vert), device_id_type=MESH_IDS)
+
+    @pl.when(row < last_row)
+    def _():
+        pl.semaphore_signal(barrier, inc=1, device_id=(row + 1, gz, vert), device_id_type=MESH_IDS)
+
     speeds = [(2 * order[s] - (NVZ - 1)).astype(F32) * UNIT for s in range(3)]
     bottom_code, top_code = codes[0], codes[1]
-    zero16 = jnp.zeros((16, HALF), F32)
+    for n in range(STEPS):
+        for s in range(3):
+            F[n, s, 0:NVT] = jnp.zeros((NVT, 128), F32)
+            F[n, s, NVT + PLANE :] = jnp.zeros((NVT, 128), F32)
+    for s in range(3):
+        G[s, :, 64:128] = jnp.zeros((HALF, 64), F32)
+
+    @pl.when(row == last_row)
+    def _():
+        for n in range(STEPS):
+            for s in range(3):
+                ghR[n, s, 0] = jnp.zeros((16, HALF), F32)
+
 
     def radial_copy(n, s, h):
         step = 1 if h else -1
@@ -331,20 +344,28 @@
 
     over_lanes = (((1,), (1,)), ((), ()))
 
+    def keep_traces(n, s, h, both):
+        trR[n, s, h] = both[0:16]
+        trA[n, s, :, h * HALF : (h + 1) * HALF] = both[16:24]
+
     def traces(n, s):
         for h in range(2):
-            here = pl.ds(h * HALF, HALF)
-            both = lax.dot_general(
-                trace[gz, h], X[s, here, 0:128], over_lanes, preferred_element_type=F32
+            x = F[n % 2, s, NVT + h * HALF : NVT + (h + 1) * HALF, :].astype(BF16)
+            both = lax.dot_general(trace[gz, h], x, over_lanes, preferred_element_type=F32)
+            keep_traces(n, s, h, both)
+
+    def plane_sums(n, s):
+        total = jnp.zeros((16, 256), F32)
+        for c in range(PLANE // 256):
+            x = F[n % 2, s, NVT + c * 256 : NVT + (c + 1) * 256, :]
+            hi = x.astype(BF16)
+            lo = (x - hi.astype(F32)).astype(BF16)
+            total += jnp.dot(
+                basis[:, c * 256 : (c + 1) * 256],
+                jnp.concatenate([hi, lo], axis=1),
+                preferred_element_type=F32,
             )
-            trR[n, s, h] = both[0:16]
-            trA[n, s, :, here] = both[16:24]
-
-    def ghost_columns(s, h, table):
-        for k in range(HALF // 128):
-            X[s, h * HALF + k * 128 : h * HALF + (k + 1) * 128, 128:160] = (
-                table[:, k * 128 : (k + 1) * 128].T.astype(BF16)
-            )
+        return combine(s, total)
 
     def ghosts(n, s):
         @pl.when(row < last_row)
@@ -355,35 +376,29 @@
         def _():
             radial_copy(n, s, 1).wait_recv()
 
-        axial_copy(n, s).wait_recv()
-        spare = jnp.zeros((8, HALF), F32)
-        low = [ghA[n, s, :, 0:HALF], spare]
-        high = [ghA[n, s, :, HALF:PLANE], spare]
-
-        @pl.when(row < last_row)
-        def _():
-            ghost_columns(s, 0, jnp.concatenate([ghR[n, s, 0]] + low, axis=0))
-
-        @pl.when(row == last_row)
-        def _():
-            ghost_columns(s, 0, jnp.concatenate([zero16] + low, axis=0))
-
-        @pl.when(row > 0)
-        def _():
-            ghost_columns(s, 1, jnp.concatenate([ghR[n, s, 1]] + high, axis=0))
-
         @pl.when(row == 0)
         def _():
             own = trR[n, s, 0]
-            mirror = jnp.concatenate(
+            ghR[n, s, 1] = jnp.concatenate(
                 [own[:, k * NVT : (k + 1) * NVT] for k in reversed(range(NVR // 2))], axis=1
             )
-            ghost_columns(s, 1, jnp.concatenate([mirror] + high, axis=0))
-
-    def plane_sums(s):
-        table = jnp.dot(basis[...], X[s, :, 0:128], preferred_element_type=F32)
-        table += jnp.dot(basis[...], LO[s], preferred_element_type=F32)
-        z = speeds[s]
+
+        axial_copy(n, s).wait_recv()
+        spare = jnp.zeros((8, 128), F32)
+
+        def turn(k, carry):
+            low = pl.ds(pl.multiple_of(k * 128, 128), 128)
+            high = pl.ds(pl.multiple_of(HALF + k * 128, 128), 128)
+            table = [ghR[n, s, 0, :, low], ghA[n, s, :, low], spare]
+            table += [ghR[n, s, 1, :, low], ghA[n, s, :, high], spare]
+            G[s, low, 0:64] = jnp.concatenate(table, axis=0).T
+            return carry
+
+        lax.fori_loop(0, HALF // 128, turn, 0, unroll=9)
+
+    def combine(s, total):
+        table = total[:, 0:128] + total[:, 128:256]
+        z = (2 * order[s] - (NVZ - 1)).astype(F32) * UNIT
         g = [table[i : i + 1] for i in range(15)]
         b0, br, bt = g[0], UNIT * g[1], UNIT * g[2]
         brr, btt, brt = (UNIT**2 * (g[i] + g[i + 1]) for i in (3, 5, 7))
@@ -407,7 +422,7 @@
 
     def send_sums(n, parts):
         for i in range(14):
-            mine[n, i : i + 1] = parts[0][i] + (parts[1][i] + parts[2][i])
+            mine[n, i : i + 1] = parts[i]
         mine[n, 14:16] = jnp.zeros((2, 128), F32)
         ARB[n, vert] = mine[n]
         each_peer(lambda peer, k: sum_copy(n, vert, peer, k).start())
@@ -473,34 +488,40 @@
                 inward * wall_gain * jnp.exp(jnp.zeros((1, 128), F32) - 0.5 * z * z)
             )
 
-    for n in range(STEPS):
-        for s in range(3):
-            F[n, s, 0:NVT] = jnp.zeros((NVT, 128), F32)
-            F[n, s, NVT + PLANE :] = jnp.zeros((NVT, 128), F32)
     for copy in consts[:2]:
         copy.wait()
-    parts = []
-    for s in range(3):
-        loads[s].wait()
-
-        def split(r, carry, s=s):
-            at = pl.ds(pl.multiple_of(r * 128, 128), 128)
-            x = RAW[s, :, at].T
-            F[0, s, pl.ds(pl.multiple_of(NVT + r * 128, 8), 128), :] = x
-            hi = x.astype(BF16)
-            X[s, at, 0:128] = hi
-            LO[s, at, :] = (x - hi.astype(F32)).astype(BF16)
-            return carry
-
-        lax.fori_loop(0, PLANE // 128, split, 0, unroll=3)
-        traces(0, s)
-        if s == 0:
+    nothing = tuple(jnp.zeros((1, 128), F32) for _ in range(14))
+
+    def add(parts, more):
+        return tuple(a + b for a, b in zip(parts, more))
+
+    def begin(s, parts):
+        load(s).wait()
+        for h in range(2):
+            lanes = slice(h * HALF, (h + 1) * HALF)
+            keep_traces(0, s, h, jnp.dot(
+                trace[gz, h], RAW[s, :, lanes].astype(BF16), preferred_element_type=F32
+            ))
+
+        @pl.when(s == 0)
+        def _():
             peers = vert_total + (row > 0).astype(jnp.int32) + (row < last_row).astype(jnp.int32)
             pl.semaphore_wait(barrier, peers)
 
-        send_halo(0, s)
-        parts.append(plane_sums(s))
-    send_sums(0, parts)
+        @pl.when(s < 2)
+        def _():
+            send_halo(0, s)
+
+        def split(r, carry):
+            at = pl.ds(pl.multiple_of(r * 128, 128), 128)
+            F[0, s, pl.ds(pl.multiple_of(NVT + r * 128, 8), 128), :] = RAW[s, :, at].T
+            return carry
+
+        lax.fori_loop(0, PLANE // 128, split, 0, unroll=9)
+        return add(parts, plane_sums(0, s))
+
+    send_sums(0, lax.fori_loop(0, 3, begin, nothing))
+    send_halo(0, 2)
 
     for copy in consts[2:]:
         copy.wait()
@@ -510,7 +531,9 @@
         down = jnp.where(gz == 0, axial[2], jnp.where(top_code == 2, axial[4], axial[3]))
         along = (z * jnp.where(z > 0, up, down)).astype(BF16)
         for h in range(2):
-            W[s, h, :, 128:256] = along
+            W[s, h, 0:128, 128:256] = along[0:128]
+            W[s, h, 128:256, 128:256] = jnp.zeros((128, 128), BF16)
+            W[s, h, 128 + 32 * h : 160 + 32 * h, 128:256] = along[128:160]
         W[s, 0, :, 0:128] = radial[jnp.where(row == last_row, 1, 0)]
         W[s, 1, :, 0:128] = radial[2]
 
@@ -519,19 +542,27 @@
         TURN[k] = rows[2 + k] * inverse
 
     for n in range(STEPS):
-        for s in range(3):
+        def move(s, none, n=n):
             ghosts(n, s)
+
             for h in range(2):
-                here = pl.ds(h * HALF, HALF)
-                TOUT[s, here, :] = jnp.dot(X[s, here, :], W[s, h], preferred_element_type=F32)
-
-            def stream(a, carry, s=s):
+                x = F[n, s, NVT + h * HALF : NVT + (h + 1) * HALF, :].astype(BF16)
+                operand = jnp.concatenate([x, G[s].astype(BF16)], axis=1)
+                TOUT[s, pl.ds(h * HALF, HALF), :] = jnp.dot(
+                    operand, W[s, h], preferred_element_type=F32
+                )
+
+            def stream(a, carry):
                 at = pl.ds(pl.multiple_of(a * NVT, 16), NVT)
-                behind, here, ahead = (
-                    F[n, s, pl.ds(pl.multiple_of((a + k) * NVT, 8), NVT), :] for k in range(3)
+                behind, ahead = (
+                    F[n, s, pl.ds(pl.multiple_of((a + k) * NVT, 8), NVT), :] for k in (0, 2)
                 )
                 speed = (2 * a - (NVR - 1)).astype(F32) * UNIT
-                around = TURN[1] * pltpu.roll(here, NVT - 1, 0) - TURN[2] * pltpu.roll(here, 1, 0)
+                base = (a + 1) * NVT
+                around = (
+                    TURN[1] * F[n, s, pl.ds(base + 1, NVT), :]
+                    - TURN[2] * F[n, s, pl.ds(base - 1, NVT), :]
+                )
                 PART[s, at, :] = (
                     TURN[0] * (ahead - behind)
                     + speed * (around + TOUT[s, at, 0:128])
@@ -540,40 +571,43 @@
                 return carry
 
             lax.fori_loop(0, NVR, stream, 0, unroll=4)
-
+            return none
+
+        lax.fori_loop(0, 3, move, 0)
         params(wait_totals(n))
 
-        parts = []
-        for s in range(3):
-
-            def update(a, carry, s=s):
+        def renew(s, parts, n=n):
+            def update(a, carry):
                 at = pl.ds(pl.multiple_of(a * NVT, 16), NVT)
                 own = pl.ds(pl.multiple_of((a + 1) * NVT, 8), NVT)
                 peak, heat, excess, wall_row = (BYR[s, k, pl.ds(a, 1), :] for k in range(4))
                 goal = (BYT[0] * peak) * (1.0 + (BYT[1] + heat) * (BYT[2] + excess))
-                x = PR[0:1] * F[n, s, own, :] + PART[s, at, :] + wall_row * rows[1] + goal
-                F[(n + 1) % 2, s, own, :] = x
-                hi = x.astype(BF16)
-                X[s, at, 0:128] = hi
-                LO[s, at, :] = (x - hi.astype(F32)).astype(BF16)
+                F[(n + 1) % 2, s, own, :] = (
+                    PR[0:1] * F[n, s, own, :] + PART[s, at, :] + wall_row * rows[1] + goal
+                )
                 return carry
 
             lax.fori_loop(0, NVR, update, 0, unroll=4)
             if n + 1 < STEPS:
                 traces(n + 1, s)
-                send_halo(n + 1, s)
-            parts.append(plane_sums(s))
-        send_sums(n + 1, parts)
-
-    for s in range(3):
-
-        def back(r, carry, s=s):
-            at = pl.ds(pl.multiple_of(r * 128, 128), 128)
+
+                @pl.when(s < 2)
+                def _():
+                    send_halo(n + 1, s)
+
+            return add(parts, plane_sums(n + 1, s))
+
+        send_sums(n + 1, lax.fori_loop(0, 3, renew, nothing))
+        if n + 1 < STEPS:
+            send_halo(n + 1, 2)
+
+    def back(r, carry):
+        for s in range(3):
             x = F[STEPS % 2, s, pl.ds(pl.multiple_of(NVT + r * 128, 8), 128), :]
             out[:, pl.ds(pl.multiple_of(s * PLANE + r * 128, 128), 128)] = x.T
-            return carry
-
-        lax.fori_loop(0, PLANE // 128, back, 0, unroll=3)
+        return carry
+
+    lax.fori_loop(0, PLANE // 128, back, 0, unroll=3)
     S = wait_totals(STEPS)
     density, u, temp, heat = observables(S)
     for i, value in enumerate([density] + u + [temp] + heat):
@@ -642,11 +676,10 @@
             scratch_shapes=[
                 pltpu.VMEM((3, 128, PLANE), F32),
                 pltpu.VMEM((2, 3, PLANE + 2 * NVT, 128), F32),
-                pltpu.VMEM((3, PLANE, 160), BF16),
-                pltpu.VMEM((3, PLANE, 128), BF16),
+                pltpu.VMEM((3, HALF, 128), F32),
                 pltpu.VMEM((3, PLANE, 128), F32),
                 pltpu.VMEM((3, PLANE, 256), F32),
-                pltpu.VMEM((3, 2, 160, 256), BF16),
+                pltpu.VMEM((3, 2, 256, 256), BF16),
                 pltpu.VMEM((3, NVT, 128), F32),
                 pltpu.VMEM((3, NVT, 128), F32),
                 pltpu.VMEM((3, 4, NVR, 128), F32),

time: 42.7 us -> 40.8 us (0.956)
  Pallas kernels: 41.9 us -> 39.9 us
    pallas_call x1, Pallas kernels: 39.3 us -> 37.3 us  [on_device(): pl.pallas_call(functools.partial(kernel, (row_total, vert_total), weight,...]
where the time goes in v3:
time: 40.8 us; the launch traced here: 40.6 us
  Pallas kernels  39.9 us (98%)
  between operations  0.64 us (2%)
    pallas_call x1, Pallas kernels, on_device(): pl.pallas_call(functools.partial(kernel, (row_total, vert_total), weight,...  37.3 us
    pallas_call x1, Pallas kernels, on_device(): pl.pallas_call(deliver, out_shape=outs, in_specs=[vmem, vmem, vmem], out_...  2.58 us

profile of v3, /device:TPU:1, one launch (start us, length us, event | category | flops | bytes accessed | tf_op | source)
XLA Modules:
  0.0 40.6 jit_solution(14207334831761326201)
XLA Ops:
  0.6 37.3 %shard_map.121 = (f32[128,6912]{1,0:T(8,128)S(1)}, f32[8,8,16]{2,1,0:T(8,128)}, f32[1,8]{1,0:T(1,128)}) custom-call(f32[128,6912]{1,0:T(8,128)} %bitcast.3, s32[3]{0:T(128)} %order.1, s32[2]{0:T(128)} %bitcast.4, bf16[3,256,128]{2,1,0:T(8,128)(2,1)} %constant.14.clone.radial_hbm, f32[5,160,128]{2,1,0:T(8,128)} %constant.15.clone.axial_hbm, ...), custom_call_target="tpu_custom_call" | custom-call | tf_op jit(solution)/shard_map/pallas_call | solution.py:671
  38.0 2.6 %shard_map.122 = (f32[128,6912]{1,0:T(8,128)}, f32[8,8,16]{2,1,0:T(8,128)}, f32[1,8]{1,0:T(1,128)}) custom-call(f32[128,6912]{1,0:T(8,128)S(1)} %get-tuple-element.9.new, f32[8,8,16]{2,1,0:T(8,128)} %get-tuple-element.10.macro, f32[1,8]{1,0:T(1,128)} %get-tuple-element.11.flux), custom_call_target="tpu_custom_call" | custom-call | tf_op jit(solution)/shard_map/pallas_call | solution.py:710

commit v4 on v3

--- a/solution.py
+++ b/solution.py
@@ -329,7 +329,7 @@
             action(lax.rem(vert + k, vert_total), k)
             return carry
 
-        lax.fori_loop(1, vert_total, body, 0)
+        lax.fori_loop(1, vert_total, body, 0, unroll=5)
 
     def send_halo(n, s):
         @pl.when(row > 0)
@@ -570,7 +570,7 @@
                 )
                 return carry
 
-            lax.fori_loop(0, NVR, stream, 0, unroll=4)
+            lax.fori_loop(0, NVR, stream, 0, unroll=8)
             return none
 
         lax.fori_loop(0, 3, move, 0)
@@ -587,7 +587,7 @@
                 )
                 return carry
 
-            lax.fori_loop(0, NVR, update, 0, unroll=4)
+            lax.fori_loop(0, NVR, update, 0, unroll=8)
             if n + 1 < STEPS:
                 traces(n + 1, s)
 

time: 40.8 us -> 40.2 us (0.985)
  Pallas kernels: 39.9 us -> 39.4 us
    pallas_call x1, Pallas kernels: 37.3 us -> 36.8 us  [on_device(): pl.pallas_call(functools.partial(kernel, (row_total, vert_total), weight,...]
where the time goes in v4:
time: 40.2 us; the launch traced here: 40 us
  Pallas kernels  39.4 us (98%)
  between operations  0.64 us (2%)
    pallas_call x1, Pallas kernels, on_device(): pl.pallas_call(functools.partial(kernel, (row_total, vert_total), weight,...  36.8 us
    pallas_call x1, Pallas kernels, on_device(): pl.pallas_call(deliver, out_shape=outs, in_specs=[vmem, vmem, vmem], out_...  2.58 us

profile of v4, /device:TPU:1, one launch (start us, length us, event | category | flops | bytes accessed | tf_op | source)
XLA Modules:
  0.0 40.0 jit_solution(3391415753799412755)
XLA Ops:
  0.6 36.8 %shard_map.121 = (f32[128,6912]{1,0:T(8,128)S(1)}, f32[8,8,16]{2,1,0:T(8,128)}, f32[1,8]{1,0:T(1,128)}) custom-call(f32[128,6912]{1,0:T(8,128)} %bitcast.3, s32[3]{0:T(128)} %order.1, s32[2]{0:T(128)} %bitcast.4, bf16[3,256,128]{2,1,0:T(8,128)(2,1)} %constant.14.clone.radial_hbm, f32[5,160,128]{2,1,0:T(8,128)} %constant.15.clone.axial_hbm, ...), custom_call_target="tpu_custom_call" | custom-call | tf_op jit(solution)/shard_map/pallas_call | solution.py:671
  37.5 2.6 %shard_map.122 = (f32[128,6912]{1,0:T(8,128)}, f32[8,8,16]{2,1,0:T(8,128)}, f32[1,8]{1,0:T(1,128)}) custom-call(f32[128,6912]{1,0:T(8,128)S(1)} %get-tuple-element.9.new, f32[8,8,16]{2,1,0:T(8,128)} %get-tuple-element.10.macro, f32[1,8]{1,0:T(1,128)} %get-tuple-element.11.flux), custom_call_target="tpu_custom_call" | custom-call | tf_op jit(solution)/shard_map/pallas_call | solution.py:710

commit v5 on v4

--- a/solution.py
+++ b/solution.py
@@ -284,7 +284,7 @@
             F[n, s, 0:NVT] = jnp.zeros((NVT, 128), F32)
             F[n, s, NVT + PLANE :] = jnp.zeros((NVT, 128), F32)
     for s in range(3):
-        G[s, :, 64:128] = jnp.zeros((HALF, 64), F32)
+        G[s, :, 64:128] = jnp.zeros((HALF, 64), BF16)
 
     @pl.when(row == last_row)
     def _():
@@ -329,7 +329,7 @@
             action(lax.rem(vert + k, vert_total), k)
             return carry
 
-        lax.fori_loop(1, vert_total, body, 0, unroll=5)
+        lax.fori_loop(1, vert_total, body, 0, unroll=15)
 
     def send_halo(n, s):
         @pl.when(row > 0)
@@ -391,7 +391,7 @@
             high = pl.ds(pl.multiple_of(HALF + k * 128, 128), 128)
             table = [ghR[n, s, 0, :, low], ghA[n, s, :, low], spare]
             table += [ghR[n, s, 1, :, low], ghA[n, s, :, high], spare]
-            G[s, low, 0:64] = jnp.concatenate(table, axis=0).T
+            G[s, low, 0:64] = jnp.concatenate(table, axis=0).T.astype(BF16)
             return carry
 
         lax.fori_loop(0, HALF // 128, turn, 0, unroll=9)
@@ -547,7 +547,7 @@
 
             for h in range(2):
                 x = F[n, s, NVT + h * HALF : NVT + (h + 1) * HALF, :].astype(BF16)
-                operand = jnp.concatenate([x, G[s].astype(BF16)], axis=1)
+                operand = jnp.concatenate([x, G[s]], axis=1)
                 TOUT[s, pl.ds(h * HALF, HALF), :] = jnp.dot(
                     operand, W[s, h], preferred_element_type=F32
                 )
@@ -570,7 +570,7 @@
                 )
                 return carry
 
-            lax.fori_loop(0, NVR, stream, 0, unroll=8)
+            lax.fori_loop(0, NVR, stream, 0, unroll=16)
             return none
 
         lax.fori_loop(0, 3, move, 0)
@@ -587,7 +587,7 @@
                 )
                 return carry
 
-            lax.fori_loop(0, NVR, update, 0, unroll=8)
+            lax.fori_loop(0, NVR, update, 0, unroll=16)
             if n + 1 < STEPS:
                 traces(n + 1, s)
 
@@ -676,7 +676,7 @@
             scratch_shapes=[
                 pltpu.VMEM((3, 128, PLANE), F32),
                 pltpu.VMEM((2, 3, PLANE + 2 * NVT, 128), F32),
-                pltpu.VMEM((3, HALF, 128), F32),
+                pltpu.VMEM((3, HALF, 128), BF16),
                 pltpu.VMEM((3, PLANE, 128), F32),
                 pltpu.VMEM((3, PLANE, 256), F32),
                 pltpu.VMEM((3, 2, 256, 256), BF16),

time: 40.2 us -> 40 us (level)
  no operation moved by 1% of the time
where the time goes in v5:
time: 40 us; the launch traced here: 39.8 us
  Pallas kernels  39.2 us (98%)
  between operations  0.64 us (2%)
    pallas_call x1, Pallas kernels, on_device(): pl.pallas_call(functools.partial(kernel, (row_total, vert_total), weight,...  36.6 us
    pallas_call x1, Pallas kernels, on_device(): pl.pallas_call(deliver, out_shape=outs, in_specs=[vmem, vmem, vmem], out_...  2.58 us

profile of v5, /device:TPU:1, one launch (start us, length us, event | category | flops | bytes accessed | tf_op | source)
XLA Modules:
  0.0 39.8 jit_solution(8230842456474183304)
XLA Ops:
  0.6 36.6 %shard_map.121 = (f32[128,6912]{1,0:T(8,128)S(1)}, f32[8,8,16]{2,1,0:T(8,128)}, f32[1,8]{1,0:T(1,128)}) custom-call(f32[128,6912]{1,0:T(8,128)} %bitcast.3, s32[3]{0:T(128)} %order.1, s32[2]{0:T(128)} %bitcast.4, bf16[3,256,128]{2,1,0:T(8,128)(2,1)} %constant.14.clone.radial_hbm, f32[5,160,128]{2,1,0:T(8,128)} %constant.15.clone.axial_hbm, ...), custom_call_target="tpu_custom_call" | custom-call | tf_op jit(solution)/shard_map/pallas_call | solution.py:671
  37.2 2.6 %shard_map.122 = (f32[128,6912]{1,0:T(8,128)}, f32[8,8,16]{2,1,0:T(8,128)}, f32[1,8]{1,0:T(1,128)}) custom-call(f32[128,6912]{1,0:T(8,128)S(1)} %get-tuple-element.9.new, f32[8,8,16]{2,1,0:T(8,128)} %get-tuple-element.10.macro, f32[1,8]{1,0:T(1,128)} %get-tuple-element.11.flux), custom_call_target="tpu_custom_call" | custom-call | tf_op jit(solution)/shard_map/pallas_call | solution.py:710

commit v6 on v5

--- a/solution.py
+++ b/solution.py
@@ -351,8 +351,8 @@
     def traces(n, s):
         for h in range(2):
             x = F[n % 2, s, NVT + h * HALF : NVT + (h + 1) * HALF, :].astype(BF16)
-            both = lax.dot_general(trace[gz, h], x, over_lanes, preferred_element_type=F32)
-            keep_traces(n, s, h, both)
+            both = lax.dot_general(x, trace[gz, h], over_lanes, preferred_element_type=F32)
+            keep_traces(n, s, h, both.T)
 
     def plane_sums(n, s):
         total = jnp.zeros((16, 256), F32)
@@ -517,7 +517,7 @@
             F[0, s, pl.ds(pl.multiple_of(NVT + r * 128, 8), 128), :] = RAW[s, :, at].T
             return carry
 
-        lax.fori_loop(0, PLANE // 128, split, 0, unroll=9)
+        lax.fori_loop(0, PLANE // 128, split, 0, unroll=18)
         return add(parts, plane_sums(0, s))
 
     send_sums(0, lax.fori_loop(0, 3, begin, nothing))

time: 40 us -> 40.2 us (level)
  no operation moved by 1% of the time
where the time goes in v6:
time: 40.2 us; the launch traced here: 40.1 us
  Pallas kernels  39.4 us (98%)
  between operations  0.64 us (2%)
    pallas_call x1, Pallas kernels, on_device(): pl.pallas_call(functools.partial(kernel, (row_total, vert_total), weight,...  36.8 us
    pallas_call x1, Pallas kernels, on_device(): pl.pallas_call(deliver, out_shape=outs, in_specs=[vmem, vmem, vmem], out_...  2.58 us

profile of v6, /device:TPU:1, one launch (start us, length us, event | category | flops | bytes accessed | tf_op | source)
XLA Modules:
  0.0 40.1 jit_solution(11159243676349699791)
XLA Ops:
  0.6 36.8 %shard_map.121 = (f32[128,6912]{1,0:T(8,128)S(1)}, f32[8,8,16]{2,1,0:T(8,128)}, f32[1,8]{1,0:T(1,128)}) custom-call(f32[128,6912]{1,0:T(8,128)} %bitcast.3, s32[3]{0:T(128)} %order.1, s32[2]{0:T(128)} %bitcast.4, bf16[3,256,128]{2,1,0:T(8,128)(2,1)} %constant.14.clone.radial_hbm, f32[5,160,128]{2,1,0:T(8,128)} %constant.15.clone.axial_hbm, ...), custom_call_target="tpu_custom_call" | custom-call | tf_op jit(solution)/shard_map/pallas_call | solution.py:671
  37.5 2.6 %shard_map.122 = (f32[128,6912]{1,0:T(8,128)}, f32[8,8,16]{2,1,0:T(8,128)}, f32[1,8]{1,0:T(1,128)}) custom-call(f32[128,6912]{1,0:T(8,128)S(1)} %get-tuple-element.9.new, f32[8,8,16]{2,1,0:T(8,128)} %get-tuple-element.10.macro, f32[1,8]{1,0:T(1,128)} %get-tuple-element.11.flux), custom_call_target="tpu_custom_call" | custom-call | tf_op jit(solution)/shard_map/pallas_call | solution.py:710
